TPU v7x, 512 devices: a whole 4x4x16 slice. The times are simulated.
512 devices in a mesh: dp: 64 (over y, z_lo, core), mp: 8 (over x, z_hi).
Axes of the slice: x: 4, y: 4, z: 16 (z_hi: 2, z_lo: 8; z = z_hi * 8 + z_lo), core: 2. Of those that a mesh axis runs over, the one named last changes fastest.
Arguments:
- activations: bfloat16 [65536, 8192], P('dp', 'mp'), may hold values from -400 to 400, as said below
- gradient: bfloat16 [8192, 8192], P('mp', 'dp'), may hold values from -250 to 250
- out_scale: float32 [8192], P('dp'), may hold values from 0.3 to 3
Outputs:
- update: bfloat16 [8192, 8192], P('mp', 'dp')
Inputs may be any that keep to these rules, and one draw needn't show every extreme that they name: activations entering the projection.
All inputs are finite; a program needn't handle non-finite values. Where the computation divides by a largest or mean magnitude, that divisor is 1e-20 or more.
Results may differ from a plain program's by a relative error of at most 0.001.
Values sent between devices are 32-bit elements; how exact they have to be, the bound alone decides.
No kernel may reach another device: no remote copies, remote signals or barrier semaphores. Data moves between devices by JAX's collectives and lax.ppermute only.
A program may use at most 64 MiB of HBM per device.

v0:
```python
import jax
import jax.numpy as jnp
from jax import lax
from jax.sharding import PartitionSpec as P

D = 8192
BLOCK = 1024


damping = 0.1
kl_bound = 2.0


def on_device(activations, gradient, out_scale):
    highest = lax.Precision.HIGHEST
    devices = lax.axis_size("dp")
    device_rank = lax.axis_index("dp")
    tokens, feature_count = activations.shape
    blocks = feature_count // BLOCK
    row_count = BLOCK // devices
    token_total = tokens * devices
    grouped = activations.reshape(tokens, blocks, BLOCK)
    row_start = device_rank * row_count
    identity = jnp.eye(BLOCK, dtype=jnp.float32)
    partial_sum = (
        jnp.einsum("tbr,tbc->brc", grouped, grouped, preferred_element_type=jnp.float32)
        / token_total
    )
    summed = lax.psum(partial_sum, "dp")
    factor_full = summed + damping * identity[None]
    largest = jnp.max(jnp.sum(jnp.abs(factor_full), axis=2), axis=1)
    inv_bound = (1.0 / largest)[:, None, None]
    first_full = 2.0 * inv_bound * identity[None] - inv_bound * inv_bound * factor_full
    grad_blocks = gradient.astype(jnp.float32).reshape(blocks, BLOCK, gradient.shape[1])
    own_first = lax.dynamic_slice_in_dim(first_full, row_start, row_count, 1)
    left_product = jnp.einsum("brk,bkc->brc", own_first, factor_full, precision=highest)
    product = jnp.einsum("brk,bkc->brc", left_product, first_full, precision=highest)
    second_rows = 2.0 * own_first - product
    applied = jnp.einsum(
        "brk,bkc->brc",
        lax.all_gather(second_rows, "dp", axis=1, tiled=True),
        grad_blocks,
        precision=highest,
    )
    scaled = applied.reshape(feature_count, gradient.shape[1]) * out_scale[None, :]
    local_sum = jnp.sum(scaled * gradient.astype(jnp.float32))
    alignment = lax.psum(local_sum, ("dp", "mp")) / (D * D)
    clip_factor = jnp.minimum(1.0, jnp.sqrt(kl_bound / alignment))
    return (scaled * clip_factor).astype(jnp.bfloat16)


def solution(mesh):
    return jax.shard_map(
        on_device,
        mesh=mesh,
        in_specs=(P("dp", "mp"), P("mp", "dp"), P("dp")),
        out_specs=P("mp", "dp"),
        check_vma=False,
    )
```

profile of v0, /device:TPU:1, one launch (start us, length us, event | category | flops | bytes accessed | tf_op | source)
XLA Modules:
  0.0 1110.1 jit_solution(7848226473046575346)
XLA Ops:
  6.5 0.0 copy-start
  6.5 0.0 all-reduce.2.cloned.1.call-start
  6.5 1.6 copy-done
  8.1 4.3 multiply_bitcast_fusion
  12.5 0.0 all-reduce.2.cloned.1.call-update
  12.5 0.0 all-gather.2.cloned.1.call-start
  12.6 848.0 %all-reduce.2.cloned.1.call-done = f32[1,1024,1024]{2,1,0:T(8,128)} async-done(((f32[1,1024,1024]{2,1,0:T(8,128)}), f32[1,1024,1024]{2,1,0:T(8,128)}) %all-reduce.2.cloned.1.call-update) | async-done | bytes 4194320 | tf_op jit(solution)/shard_map/psum | solution.py:29
  860.6 2.6 abs_reduce_fusion
  863.2 0.6 reduce_max.9
  864.5 0.0 copy-start.1
  864.5 2.9 multiply_subtract_fusion
  867.4 0.6 copy-done.1
  867.9 0.0 copy-start.2
  867.9 0.0 copy-start.3
  867.9 2.1 fusion.4
  870.1 2.7 fusion.14
  872.8 0.0 all-gather.2.cloned.1.call-update
  872.8 121.9 %all-gather.2.cloned.1.call-done = f32[1,1024,1024]{2,1,0:T(8,128)} async-done(((f32[1,16,1024]{2,1,0:T(8,128)}), f32[1,1024,1024]{2,1,0:T(8,128)}) %all-gather.2.cloned.1.call-update) | async-done | bytes 4194320 | tf_op jit(solution)/shard_map/all_gather | solution.py:41
  994.7 0.0 copy-done.2
  994.7 0.0 copy-done.3
  994.7 4.7 multiply_reduce_fusion
  999.5 102.3 %psum.15 = f32[]{:T(128)} all-reduce(f32[]{:T(128)} %get-tuple-element.5), channel_id=1, replica_groups=mesh['dp'=64,'mp'=8] {'dp','mp'}, use_global_device_ids=true, to_apply=%region_4.0 | all-reduce | flops 1 | bytes 8 | tf_op jit(solution)/shard_map/psum | solution.py:47
  1102.5 0.7 multiply_convert_fusion
Async XLA Ops:
  6.5 1.6 copy-start
  6.5 854.0 %all-reduce.2.cloned.1.call-start = ((), (), s32[]{:S(2)}) async-start(), calls=%async_computation | async-start | bytes 8388608 | tf_op jit(solution)/shard_map/psum | solution.py:29
  12.5 982.2 %all-gather.2.cloned.1.call-start = ((), (), s32[]{:S(2)}) async-start(), calls=%async_computation.1 | async-start | bytes 4259840 | tf_op jit(solution)/shard_map/all_gather | solution.py:41
  864.5 3.5 copy-start.1
  867.9 126.8 %copy-start.2 = (bf16[1024,128]{1,0:T(8,128)(2,1)S(1)}, bf16[1024,128]{1,0:T(8,128)(2,1)}, u32[]{:S(2)}) copy-start(bf16[1024,128]{1,0:T(8,128)(2,1)} %param.4) | copy-start | bytes 786436
  867.9 126.8 %copy-start.3 = (f32[128]{0:T(128)S(1)}, f32[128]{0:T(128)}, u32[]{:S(2)}) copy-start(f32[128]{0:T(128)} %param.5) | copy-start | bytes 1540
Sparse Core Ops, SparseCore 0:
  12.6 847.9 all-reduce.1
  873.0 121.7 all-gather.1
where the time goes:
time: 1110 us
  waiting for transfers between devices  970 us (87%)
  blocking collectives  102 us (9%)
  between operations  14.9 us (1%)
  matrix products  14 us (1%)
    psum x1, waiting for transfers between devices, on_device(): summed = lax.psum(partial_sum, 'dp')  848 us
    all_gather x1, waiting for transfers between devices, on_device(): lax.all_gather(second_rows, 'dp', axis=1, tiled=True)  122 us
    psum x1, blocking collectives, on_device(): alignment = lax.psum(local_sum, ('dp', 'mp')) / (D * D)  102 us
  transfers between devices with their start and end apart: 2, of which 2 were waited for; matrix products, arithmetic and copies ran while one was open for 0% of the time, Pallas kernels for 0%

commit v1 on v0

v1 whole, which is shorter than its diff:
```python
import functools

import jax
import jax.numpy as jnp
from jax import lax
from jax.experimental import pallas as pl
from jax.experimental.pallas import tpu as pltpu
from jax.sharding import Mesh, PartitionSpec as P

D = 8192
BLOCK = 1024
TILE = 128
HALF = 512
COLS = 128
TOKENS = 65536
SHARE = 18 * TILE

damping = 0.1
kl_bound = 2.0

AXES = ("y", "zb", "zq", "core", "x", "zh")
SIZES = (4, 2, 4, 2, 4, 2)
DP = AXES[:4]
MP = AXES[4:]

f32 = jnp.float32
bf16 = jnp.bfloat16


def gram_kernel(share_ref, own_ref, other_ref, out_ref):
    share = share_ref[0]

    def product(lhs, rhs):
        return lax.dot_general(
            lhs, rhs, (((0,), (0,)), ((), ())), preferred_element_type=f32
        )

    own = own_ref[...]
    other = other_ref[...]
    for pair in range(2):
        lhs = own[:, pair * 256 : (pair + 1) * 256]
        if pair == 0:
            wide = jnp.concatenate([own, other[:, :256]], axis=1)
        else:
            wide = jnp.concatenate([own[:, 256:], other], axis=1)
        strip = product(lhs, wide)
        for i in range(2):
            rows = strip[i * TILE : (i + 1) * TILE]
            for d in range(4):
                k = (pair * 2 + i) * 4 + d
                out_ref[k * TILE : (k + 1) * TILE, :] = rows[
                    :, (i + d) * TILE : (i + d + 1) * TILE
                ]

            @pl.when(share == pair)
            def _():
                k = 16 + i
                out_ref[k * TILE : (k + 1) * TILE, :] = rows[
                    :, (i + 4) * TILE : (i + 5) * TILE
                ]


def gram(share, activations):
    tokens = activations.shape[0]
    return pl.pallas_call(
        gram_kernel,
        out_shape=jax.ShapeDtypeStruct((SHARE, TILE), f32),
        grid_spec=pltpu.PrefetchScalarGridSpec(
            num_scalar_prefetch=1,
            grid=(1,),
            in_specs=[
                pl.BlockSpec((tokens, HALF), lambda g, s: (0, s[0])),
                pl.BlockSpec((tokens, HALF), lambda g, s: (0, 1 - s[0])),
            ],
            out_specs=pl.BlockSpec((SHARE, TILE), lambda g, s: (0, 0)),
        ),
        compiler_params=pltpu.CompilerParams(vmem_limit_bytes=24 * 2**20),
        cost_estimate=pl.CostEstimate(
            flops=2 * tokens * 512 * 768, bytes_accessed=3 * 2**20, transcendentals=0
        ),
        name="gram",
    )(share, activations, activations)


def precondition_kernel(
    share_ref,
    own_ref,
    other_ref,
    grad_lo_ref,
    grad_hi_ref,
    scale_ref,
    scaled_lo_ref,
    scaled_hi_ref,
    align_ref,
    high_ref,
    low_ref,
    sums_ref,
):
    share = share_ref[0]
    eye = lax.broadcasted_iota(jnp.int32, (TILE, TILE), 0) == lax.broadcasted_iota(
        jnp.int32, (TILE, TILE), 1
    )
    sums_ref[...] = jnp.zeros_like(sums_ref)

    def put(tile, i, j):
        high = tile.astype(bf16)
        low = (tile - high.astype(f32)).astype(bf16)
        at = (slice(i * TILE, (i + 1) * TILE), slice(j * TILE, (j + 1) * TILE))
        high_ref[at] = high
        low_ref[at] = low
        part = jnp.abs(tile).reshape(16, 8, TILE)
        sums_ref[:, j * TILE : (j + 1) * TILE] += jnp.sum(part, axis=0)

    def place(ref, k, i, j):
        tile = ref[k * TILE : (k + 1) * TILE, :] * (1.0 / TOKENS)
        if i == j:
            put(tile + jnp.where(eye, damping, 0.0), i, j)
        else:
            put(tile, i, j)
            put(tile.T, j, i)

    for base, ref in ((0, own_ref), (4, other_ref)):
        for i in range(4):
            for d in range(4):
                place(ref, i * 4 + d, base + i, (base + i + d) % 8)
    for core in range(2):

        @pl.when(share == core)
        def _():
            for i in range(2):
                row = 2 * core + i
                place(own_ref, 16 + i, row, row + 4)
                row = 2 * (1 - core) + i
                place(other_ref, 16 + i, row + 4, row)

    bound = 1.0 / jnp.max(jnp.sum(sums_ref[...], axis=0, keepdims=True), axis=1, keepdims=True)
    bound2 = bound * bound
    high = high_ref[...]
    low = low_ref[...]

    def dot(a, b):
        return jnp.dot(a, b, preferred_element_type=f32)

    def times(v):
        v_high = v.astype(bf16)
        v_low = (v - v_high.astype(f32)).astype(bf16)
        both = dot(high, jnp.concatenate([v_high, v_low], axis=1))
        return both[:, :COLS] + (both[:, COLS:] + dot(low, v_high))

    grad16 = jnp.concatenate([grad_lo_ref[...], grad_hi_ref[...]], axis=0)
    grad = grad16.astype(f32)
    u = 2.0 * bound * grad - bound2 * (dot(high, grad16) + dot(low, grad16))
    v = times(u)
    applied = 2.0 * u - (2.0 * bound * v - bound2 * times(v))
    scaled = applied * scale_ref[...]
    scaled_lo_ref[...] = scaled[:HALF]
    scaled_hi_ref[...] = scaled[HALF:]
    local = jnp.sum(scaled * grad, axis=0, keepdims=True)
    align_ref[...] = jnp.broadcast_to(local[None], align_ref.shape)


def precondition(share, own, other, gradient, out_scale, copies):
    whole = lambda g, s: (0, 0)
    half = jax.ShapeDtypeStruct((HALF, COLS), f32)
    return pl.pallas_call(
        precondition_kernel,
        out_shape=(half, half, jax.ShapeDtypeStruct((copies, 1, COLS), f32)),
        grid_spec=pltpu.PrefetchScalarGridSpec(
            num_scalar_prefetch=1,
            grid=(1,),
            in_specs=[
                pl.BlockSpec((SHARE, TILE), whole),
                pl.BlockSpec((SHARE, TILE), whole),
                pl.BlockSpec((HALF, COLS), lambda g, s: (s[0], 0)),
                pl.BlockSpec((HALF, COLS), lambda g, s: (1 - s[0], 0)),
                pl.BlockSpec((1, COLS), whole),
            ],
            out_specs=(
                pl.BlockSpec((HALF, COLS), whole),
                pl.BlockSpec((HALF, COLS), whole),
                pl.BlockSpec((copies, 1, COLS), lambda g, s: (0, 0, 0)),
            ),
            scratch_shapes=[
                pltpu.VMEM((BLOCK, BLOCK), bf16),
                pltpu.VMEM((BLOCK, BLOCK), bf16),
                pltpu.VMEM((8, BLOCK), f32),
            ],
        ),
        compiler_params=pltpu.CompilerParams(vmem_limit_bytes=40 * 2**20),
        cost_estimate=pl.CostEstimate(
            flops=2 * 9 * BLOCK * BLOCK * COLS, bytes_accessed=4 * 2**20, transcendentals=0
        ),
        name="precondition",
    )(share, own, other, gradient, gradient, out_scale.reshape(1, COLS))


def clip_kernel(share_ref, lo_ref, hi_ref, align_ref, out_ref):
    share = share_ref[0]
    lanes = jnp.sum(align_ref[...], axis=0)
    alignment = jnp.sum(lanes, axis=1, keepdims=True) * (1.0 / (D * D))
    factor = jnp.minimum(1.0, jnp.sqrt(kl_bound / alignment))
    for core in range(2):

        @pl.when(share == core)
        def _():
            first, last = (lo_ref, hi_ref) if core == 0 else (hi_ref, lo_ref)
            out_ref[:HALF, :] = (first[...] * factor).astype(bf16)
            out_ref[HALF:, :] = (last[...] * factor).astype(bf16)


def clip(share, lo, hi, align):
    vmem = pl.BlockSpec(memory_space=pltpu.VMEM)
    return pl.pallas_call(
        clip_kernel,
        out_shape=jax.ShapeDtypeStruct((BLOCK, COLS), bf16),
        in_specs=[pl.BlockSpec(memory_space=pltpu.SMEM), vmem, vmem, vmem],
        out_specs=vmem,
        cost_estimate=pl.CostEstimate(
            flops=2 * BLOCK * COLS, bytes_accessed=2**20, transcendentals=0
        ),
        name="clip",
    )(share, lo, hi, align)


def swap_cores(x):
    return lax.ppermute(x, "core", [(0, 1), (1, 0)])


def scatter_sum(x, axes, parts):
    pieces = x.reshape(parts, x.shape[0] // parts, x.shape[1])
    return jnp.sum(lax.all_to_all(pieces, axes, 0, 0), axis=0)


def gather(x, axes, parts):
    copies = jnp.broadcast_to(x[None], (parts, *x.shape))
    return lax.all_to_all(copies, axes, 0, 0).reshape(parts * x.shape[0], x.shape[1])


def on_device(activations, gradient, out_scale):
    core = lax.axis_index("core").astype(jnp.int32)
    mine = core.reshape(1)
    theirs = 1 - mine
    away = swap_cores(gram(theirs, activations))
    chip = gram(mine, activations) + away
    part = scatter_sum(chip, ("y",), 4)
    part = scatter_sum(part, ("zb", "zq"), 8)
    part = gather(part, ("zb", "zq"), 8)
    own = gather(part, ("y",), 4)
    other = swap_cores(own)
    lo, hi, align = precondition(mine, own, other, gradient, out_scale, 32)
    lanes = jnp.sum(lax.all_to_all(align, ("y", "core", "x"), 0, 0), axis=0)
    lanes = jnp.broadcast_to(lanes[None], (16, 1, COLS))
    lanes = lax.all_to_all(lanes, ("zb", "zq", "zh"), 0, 0)
    return clip(mine, lo, hi, lanes)


def solution(mesh):
    fine = Mesh(mesh.devices.reshape(SIZES), AXES)
    return jax.shard_map(
        on_device,
        mesh=fine,
        in_specs=(P(DP, MP), P(MP, DP), P(DP)),
        out_specs=P(MP, DP),
        check_vma=False,
    )
```

time: 1110 us -> 146 us (0.13)
  waiting for transfers between devices: 970 us -> 3.31 us
  starting transfers between devices: 0.04 us -> 15.4 us
  between operations: 14.9 us -> 0.1 us
  matrix products: 14 us -> 0 us
  Pallas kernels: 0 us -> 11.6 us
    psum x1 -> x0, waiting for transfers between devices: 848 us -> none  [on_device(): summed = lax.psum(partial_sum, 'dp')]
    all_gather x1 -> x0, waiting for transfers between devices: 122 us -> none  [on_device(): lax.all_gather(second_rows, 'dp', axis=1, tiled=True)]
    all_to_all x0 -> x6, blocking collectives: none -> 112 us  [the longest x2 42.6 us: scatter_sum(): return jnp.sum(lax.all_to_all(pieces, axes, 0, 0), axis=0)]
    psum x1 -> x0, blocking collectives: 102 us -> none  [on_device(): alignment = lax.psum(local_sum, ('dp', 'mp')) / (D * D)]
    ppermute x0 -> x2, starting transfers between devices: none -> 15.4 us  [swap_cores(): return lax.ppermute(x, 'core', [(0, 1), (1, 0)])]
    dot_general x4 -> x0, matrix products: 14 us -> none  [the longest x1 4.74 us: on_device(): jnp.einsum('brk,bkc->brc', lax.all_gather(second_rows, 'dp', axis=1, tile...]
    pallas_call x0 -> x4, Pallas kernels: none -> 11.6 us  [the longest x1 6.6 us: precondition(): pl.pallas_call(precondition_kernel, out_shape=(half, half, jax.ShapeDtype...]
  transfers between devices with their start and end apart: 2 -> 2, of which waited for: 2 -> 2; matrix products, arithmetic and copies ran while one was open for 0% -> 0% of each run, Pallas kernels for 0% -> 1%
where the time goes in v1:
time: 146 us
  blocking collectives  112 us (77%)
  starting transfers between devices  15.4 us (11%)
  Pallas kernels  11.6 us (8%)
  waiting for transfers between devices  3.31 us (2%)
  local copies, waits for them, and re-layouts  3.09 us (2%)
    all_to_all x2, blocking collectives, scatter_sum(): return jnp.sum(lax.all_to_all(pieces, axes, 0, 0), axis=0)  42.6 us
    all_to_all x2, blocking collectives, gather(): lax.all_to_all(copies, axes, 0, 0).reshape(parts * x.shape[0], x.shape[1])  38.1 us
    all_to_all x1, blocking collectives, on_device(): lanes = lax.all_to_all(lanes, ('zb', 'zq', 'zh'), 0, 0)  19.4 us
    ppermute x2, starting transfers between devices, swap_cores(): return lax.ppermute(x, 'core', [(0, 1), (1, 0)])  15.4 us
    all_to_all x1, blocking collectives, on_device(): lanes = jnp.sum(lax.all_to_all(align, ('y', 'core', 'x'), 0, 0), axis=0)  12.1 us
    pallas_call x1, Pallas kernels, precondition(): pl.pallas_call(precondition_kernel, out_shape=(half, half, jax.ShapeDtype...  6.6 us
    ppermute x2, waiting for transfers between devices, swap_cores(): return lax.ppermute(x, 'core', [(0, 1), (1, 0)])  3.31 us
    pallas_call x2, Pallas kernels, gram(): pl.pallas_call(gram_kernel, out_shape=jax.ShapeDtypeStruct((SHARE, TILE),...  3.14 us
  transfers between devices with their start and end apart: 2, of which 2 were waited for; matrix products, arithmetic and copies ran while one was open for 0% of the time, Pallas kernels for 1%

profile of v1, /device:TPU:1, one launch (start us, length us, event | category | flops | bytes accessed | tf_op | source)
XLA Modules:
  0.0 146.0 jit_solution(8965057619319261334)
XLA Ops:
  0.0 1.6 %copy-done = bf16[1024,1024]{1,0:T(8,128)(2,1)S(1)} copy-done((bf16[1024,1024]{1,0:T(8,128)(2,1)S(1)}, bf16[1024,1024]{1,0:T(8,128)(2,1)}, u32[]{:S(2)}) %copy-start) | copy-done | bytes 2097176
  1.6 1.6 %gram.3 = f32[2304,128]{1,0:T(8,128)S(1)} custom-call(s32[1]{0:T(128)S(6)} %sub.3.share_ref, bf16[1024,1024]{1,0:T(8,128)(2,1)S(1)} %copy-done, bf16[1024,1024]{1,0:T(8,128)(2,1)S(1)} %copy-done), custom_call_target="tpu_custom_call" | custom-call | flops 805306368 | bytes 3145728 | tf_op jit(solution)/shard_map/gram/pallas_call | solution.py:65
  3.2 8.8 %collective-permute-start = (f32[2304,128]{1,0:T(8,128)S(1)}, f32[2304,128]{1,0:T(8,128)S(1)}, u32[]{:S(2)}, u32[]{:S(2)}) collective-permute-start(f32[2304,128]{1,0:T(8,128)S(1)} %gram.3), channel_id=1, source_target_pairs={{0,8},{8,0},{1,9},{9,1},{2,10},{10,2},{3,11},{11,3},{4,12},{12,4},... | collective-permute-start | bytes 3538952 | tf_op jit(solution)/shard_map/ppermute | solution.py:226
  12.0 1.6 %gram.2 = f32[2304,128]{1,0:T(8,128)S(1)} custom-call(s32[1]{0:T(128)} %bitcast.share_ref, bf16[1024,1024]{1,0:T(8,128)(2,1)S(1)} %copy-done.1, bf16[1024,1024]{1,0:T(8,128)(2,1)S(1)} %copy-done.1), custom_call_target="tpu_custom_call" | custom-call | flops 805306368 | bytes 3145728 | tf_op jit(solution)/shard_map/gram/pallas_call | solution.py:65
  13.6 0.9 collective-permute-done
  14.4 0.1 add.3
  14.6 18.7 %all_to_all.30 = f32[4,576,128]{2,1,0:T(8,128)S(1)} all-to-all(f32[4,576,128]{2,1,0:T(8,128)S(1)} %bitcast.9), channel_id=1, replica_groups=mesh['y'=4,'zb'=2,'zq'=4,'core'=2,'x'=4,'zh'=2] {'y'}, dimensions={0} | all-to-all | bytes 2359296 | tf_op jit(solution)/shard_map/all_to_all | solution.py:231
  33.2 0.1 reduce_sum.27
  33.3 23.9 %all_to_all.31 = f32[8,72,128]{2,1,0:T(8,128)S(1)} all-to-all(f32[8,72,128]{2,1,0:T(8,128)S(1)} %bitcast.10), channel_id=1, replica_groups=mesh['y'=4,'zb'=2,'zq'=4,'core'=2,'x'=4,'zh'=2] {'zb','zq'}, dimensions={0} | all-to-all | bytes 589824 | tf_op jit(solution)/shard_map/all_to_all | solution.py:231
  57.3 22.8 %all_to_all.32 = f32[8,72,128]{2,1,0:T(8,128)S(1)} all-to-all(f32[8,72,128]{2,1,0:T(8,128)S(1)} %broadcast_in_dim.8), channel_id=1, replica_groups=mesh['y'=4,'zb'=2,'zq'=4,'core'=2,'x'=4,'zh'=2] {'zb','zq'}, dimensions={0} | all-to-all | bytes 589824 | tf_op jit(solution)/shard_map/all_to_all | solution.py:236
  80.0 0.1 broadcast_in_dim.10
  80.1 0.0 copy-start.4
  80.1 0.0 copy-start.5
  80.2 15.3 %all_to_all.33 = f32[4,576,128]{2,1,0:T(8,128)S(1)} all-to-all(f32[4,576,128]{2,1,0:T(8,128)S(1)} %broadcast_in_dim.10), channel_id=1, replica_groups=mesh['y'=4,'zb'=2,'zq'=4,'core'=2,'x'=4,'zh'=2] {'y'}, dimensions={0} | all-to-all | bytes 2359296 | tf_op jit(solution)/shard_map/all_to_all | solution.py:236
  95.4 6.6 %collective-permute-start.1 = (f32[2304,128]{1,0:T(8,128)S(1)}, f32[2304,128]{1,0:T(8,128)S(1)}, u32[]{:S(2)}, u32[]{:S(2)}) collective-permute-start(f32[2304,128]{1,0:T(8,128)S(1)} %bitcast.6), channel_id=1, source_target_pairs={{0,8},{8,0},{1,9},{9,1},{2,10},{10,2},{3,11},{11,3},{4,12},{12,4},... | collective-permute-start | bytes 3538952 | tf_op jit(solution)/shard_map/ppermute | solution.py:226
  102.1 2.5 %collective-permute-done.1.other_ref = f32[2304,128]{1,0:T(8,128)S(1)} collective-permute-done((f32[2304,128]{1,0:T(8,128)S(1)}, f32[2304,128]{1,0:T(8,128)S(1)}, u32[]{:S(2)}, u32[]{:S(2)}) %collective-permute-start.1) | collective-permute-done | bytes 1179680 | tf_op jit(solution)/shard_map/ppermute | solution.py:226
  104.5 0.0 copy-done.5
  104.5 6.6 %precondition.1 = (f32[512,128]{1,0:T(8,128)S(1)}, f32[512,128]{1,0:T(8,128)S(1)}, f32[32,1,128]{2,1,0:T(1,128)S(1)}) custom-call(s32[1]{0:T(128)} %bitcast.share_ref, f32[2304,128]{1,0:T(8,128)S(1)} %bitcast.7, f32[2304,128]{1,0:T(8,128)S(1)} %collective-permute-done.1.other_ref, bf16[1024,128]{1,0:T(8,128)(2,1)S(1)} %copy-done.4, ...), custom_call_target="tpu_custom_call" | custom-call | flops 2415919104 | bytes 4194304 | tf_op jit(solution)/shard_map/precondition/pallas_call | solution.py:165
  111.1 0.7 copy-done.2
  111.8 0.7 copy-done.3
  112.5 12.1 %all_to_all.34 = f32[32,1,128]{2,1,0:T(1,128)S(1)} all-to-all(f32[32,1,128]{2,1,0:T(1,128)S(1)} %get-tuple-element.10), channel_id=1, replica_groups=mesh['y'=4,'zb'=2,'zq'=4,'core'=2,'x'=4,'zh'=2] {'y','core','x'}, dimensions={0} | all-to-all | bytes 32768 | tf_op jit(solution)/shard_map/all_to_all | solution.py:251
  124.7 0.1 reduce_sum.29
  124.7 19.4 %all_to_all.35.align_ref = f32[16,1,128]{2,1,0:T(1,128)} all-to-all(f32[16,1,128]{2,1,0:T(1,128)S(1)} %broadcast_in_dim.22), channel_id=1, replica_groups=mesh['y'=4,'zb'=2,'zq'=4,'core'=2,'x'=4,'zh'=2] {'zb','zq','zh'}, dimensions={0} | all-to-all | bytes 16384 | tf_op jit(solution)/shard_map/all_to_all | solution.py:253
  144.1 1.9 %clip.1 = bf16[1024,128]{1,0:T(8,128)(2,1)} custom-call(s32[1]{0:T(128)} %bitcast.share_ref, f32[512,128]{1,0:T(8,128)} %copy-done.2, f32[512,128]{1,0:T(8,128)} %copy-done.3, f32[16,1,128]{2,1,0:T(1,128)} %all_to_all.35.align_ref), custom_call_target="tpu_custom_call" | custom-call | flops 262144 | bytes 1048576 | tf_op jit(solution)/shard_map/clip/pallas_call | solution.py:213
  (9 shorter events, 0.1 us)
Async XLA Ops:
  0.0 1.6 %copy-start = (bf16[1024,1024]{1,0:T(8,128)(2,1)S(1)}, bf16[1024,1024]{1,0:T(8,128)(2,1)}, u32[]{:S(2)}) copy-start(bf16[1024,1024]{1,0:T(8,128)(2,1)} %other_ref.3) | copy-start | bytes 6291460
  1.6 10.4 %copy-start.1 = (bf16[1024,1024]{1,0:T(8,128)(2,1)S(1)}, bf16[1024,1024]{1,0:T(8,128)(2,1)}, u32[]{:S(2)}) copy-start(bf16[1024,1024]{1,0:T(8,128)(2,1)} %other_ref.3) | copy-start | bytes 6291460
  3.2 11.3 %collective-permute-start = (f32[2304,128]{1,0:T(8,128)S(1)}, f32[2304,128]{1,0:T(8,128)S(1)}, u32[]{:S(2)}, u32[]{:S(2)}) collective-permute-start(f32[2304,128]{1,0:T(8,128)S(1)} %gram.3), channel_id=1, source_target_pairs={{0,8},{8,0},{1,9},{9,1},{2,10},{10,2},{3,11},{11,3},{4,12},{12,4},... | collective-permute-start | bytes 3538952 | tf_op jit(solution)/shard_map/ppermute | solution.py:226
  80.1 24.4 %copy-start.4 = (bf16[1024,128]{1,0:T(8,128)(2,1)S(1)}, bf16[1024,128]{1,0:T(8,128)(2,1)}, u32[]{:S(2)}) copy-start(bf16[1024,128]{1,0:T(8,128)(2,1)} %grad_hi_ref.1) | copy-start | bytes 786436
  80.1 24.4 %copy-start.5 = (f32[128]{0:T(128)S(1)}, f32[128]{0:T(128)}, u32[]{:S(2)}) copy-start(f32[128]{0:T(128)} %param.5) | copy-start | bytes 1540
  95.4 9.1 %collective-permute-start.1 = (f32[2304,128]{1,0:T(8,128)S(1)}, f32[2304,128]{1,0:T(8,128)S(1)}, u32[]{:S(2)}, u32[]{:S(2)}) collective-permute-start(f32[2304,128]{1,0:T(8,128)S(1)} %bitcast.6), channel_id=1, source_target_pairs={{0,8},{8,0},{1,9},{9,1},{2,10},{10,2},{3,11},{11,3},{4,12},{12,4},... | collective-permute-start | bytes 3538952 | tf_op jit(solution)/shard_map/ppermute | solution.py:226
  111.1 0.7 copy-start.2
  111.8 0.7 copy-start.3

commit v2 on v1

--- a/solution.py
+++ b/solution.py
@@ -18,10 +18,10 @@
 damping = 0.1
 kl_bound = 2.0
 
-AXES = ("y", "zb", "zq", "core", "x", "zh")
-SIZES = (4, 2, 4, 2, 4, 2)
-DP = AXES[:4]
-MP = AXES[4:]
+AXES = ("y", "z4", "z2", "z1", "core", "x", "z8")
+SIZES = (4, 2, 2, 2, 2, 4, 2)
+DP = AXES[:5]
+MP = AXES[5:]
 
 f32 = jnp.float32
 bf16 = jnp.bfloat16
@@ -89,8 +89,7 @@
     grad_lo_ref,
     grad_hi_ref,
     scale_ref,
-    scaled_lo_ref,
-    scaled_hi_ref,
+    scaled_ref,
     align_ref,
     high_ref,
     low_ref,
@@ -153,18 +152,20 @@
     v = times(u)
     applied = 2.0 * u - (2.0 * bound * v - bound2 * times(v))
     scaled = applied * scale_ref[...]
-    scaled_lo_ref[...] = scaled[:HALF]
-    scaled_hi_ref[...] = scaled[HALF:]
+    scaled_ref[pl.ds(pl.multiple_of(share * HALF, HALF), HALF), :] = scaled[:HALF]
+    scaled_ref[pl.ds(pl.multiple_of((1 - share) * HALF, HALF), HALF), :] = scaled[HALF:]
     local = jnp.sum(scaled * grad, axis=0, keepdims=True)
     align_ref[...] = jnp.broadcast_to(local[None], align_ref.shape)
 
 
 def precondition(share, own, other, gradient, out_scale, copies):
     whole = lambda g, s: (0, 0)
-    half = jax.ShapeDtypeStruct((HALF, COLS), f32)
     return pl.pallas_call(
         precondition_kernel,
-        out_shape=(half, half, jax.ShapeDtypeStruct((copies, 1, COLS), f32)),
+        out_shape=(
+            jax.ShapeDtypeStruct((BLOCK, COLS), f32),
+            jax.ShapeDtypeStruct((copies, 1, COLS), f32),
+        ),
         grid_spec=pltpu.PrefetchScalarGridSpec(
             num_scalar_prefetch=1,
             grid=(1,),
@@ -176,8 +177,7 @@
                 pl.BlockSpec((1, COLS), whole),
             ],
             out_specs=(
-                pl.BlockSpec((HALF, COLS), whole),
-                pl.BlockSpec((HALF, COLS), whole),
+                pl.BlockSpec((BLOCK, COLS), whole),
                 pl.BlockSpec((copies, 1, COLS), lambda g, s: (0, 0, 0)),
             ),
             scratch_shapes=[
@@ -194,36 +194,29 @@
     )(share, own, other, gradient, gradient, out_scale.reshape(1, COLS))
 
 
-def clip_kernel(share_ref, lo_ref, hi_ref, align_ref, out_ref):
-    share = share_ref[0]
+def clip_kernel(scaled_ref, align_ref, out_ref):
     lanes = jnp.sum(align_ref[...], axis=0)
     alignment = jnp.sum(lanes, axis=1, keepdims=True) * (1.0 / (D * D))
     factor = jnp.minimum(1.0, jnp.sqrt(kl_bound / alignment))
-    for core in range(2):
-
-        @pl.when(share == core)
-        def _():
-            first, last = (lo_ref, hi_ref) if core == 0 else (hi_ref, lo_ref)
-            out_ref[:HALF, :] = (first[...] * factor).astype(bf16)
-            out_ref[HALF:, :] = (last[...] * factor).astype(bf16)
-
-
-def clip(share, lo, hi, align):
+    out_ref[...] = (scaled_ref[...] * factor).astype(bf16)
+
+
+def clip(scaled, align):
     vmem = pl.BlockSpec(memory_space=pltpu.VMEM)
     return pl.pallas_call(
         clip_kernel,
         out_shape=jax.ShapeDtypeStruct((BLOCK, COLS), bf16),
-        in_specs=[pl.BlockSpec(memory_space=pltpu.SMEM), vmem, vmem, vmem],
+        in_specs=[vmem, vmem],
         out_specs=vmem,
         cost_estimate=pl.CostEstimate(
             flops=2 * BLOCK * COLS, bytes_accessed=2**20, transcendentals=0
         ),
         name="clip",
-    )(share, lo, hi, align)
-
-
-def swap_cores(x):
-    return lax.ppermute(x, "core", [(0, 1), (1, 0)])
+    )(scaled, align)
+
+
+def swap(x, axis):
+    return lax.ppermute(x, axis, [(0, 1), (1, 0)])
 
 
 def scatter_sum(x, axes, parts):
@@ -240,18 +233,18 @@
     core = lax.axis_index("core").astype(jnp.int32)
     mine = core.reshape(1)
     theirs = 1 - mine
-    away = swap_cores(gram(theirs, activations))
+    away = swap(gram(theirs, activations), "core")
     chip = gram(mine, activations) + away
-    part = scatter_sum(chip, ("y",), 4)
-    part = scatter_sum(part, ("zb", "zq"), 8)
-    part = gather(part, ("zb", "zq"), 8)
-    own = gather(part, ("y",), 4)
-    other = swap_cores(own)
-    lo, hi, align = precondition(mine, own, other, gradient, out_scale, 32)
+    part = scatter_sum(chip, ("y", "z1"), 8)
+    part = part + swap(part, "z2")
+    part = part + swap(part, "z4")
+    own = gather(part, ("y", "z1"), 8)
+    other = swap(own, "core")
+    scaled, align = precondition(mine, own, other, gradient, out_scale, 32)
     lanes = jnp.sum(lax.all_to_all(align, ("y", "core", "x"), 0, 0), axis=0)
     lanes = jnp.broadcast_to(lanes[None], (16, 1, COLS))
-    lanes = lax.all_to_all(lanes, ("zb", "zq", "zh"), 0, 0)
-    return clip(mine, lo, hi, lanes)
+    lanes = lax.all_to_all(lanes, ("z4", "z2", "z1", "z8"), 0, 0)
+    return clip(scaled, lanes)
 
 
 def solution(mesh):

time: 146 us -> 134 us (0.918)
  blocking collectives: 112 us -> 72.1 us
  waiting for transfers between devices: 3.31 us -> 26.9 us
  starting transfers between devices: 15.4 us -> 19.9 us
    ppermute x2 -> x4, waiting for transfers between devices: 3.31 us -> 26.9 us  [swap(): return lax.ppermute(x, axis, [(0, 1), (1, 0)])]
    all_to_all x2 -> x1, blocking collectives: 42.6 us -> 19.3 us  [scatter_sum(): return jnp.sum(lax.all_to_all(pieces, axes, 0, 0), axis=0)]
    all_to_all x2 -> x1, blocking collectives: 38.1 us -> 19.3 us  [gather(): lax.all_to_all(copies, axes, 0, 0).reshape(parts * x.shape[0], x.shape[1])]
    ppermute x2 -> x4, starting transfers between devices: 15.4 us -> 19.9 us  [swap(): return lax.ppermute(x, axis, [(0, 1), (1, 0)])]
    all_to_all x1, blocking collectives: 19.4 us -> 22.3 us  [on_device(): lanes = lax.all_to_all(lanes, ('z4', 'z2', 'z1', 'z8'), 0, 0)]
    unnamed x12 -> x10, local copies, waits for them, and re-layouts: 2.99 us -> 2.4 us
  transfers between devices with their start and end apart: 2 -> 4, of which waited for: 2 -> 4; matrix products, arithmetic and copies ran while one was open for 0% -> 0% of each run, Pallas kernels for 1% -> 1%
where the time goes in v2:
time: 134 us; the launch traced here: 133 us
  blocking collectives  72.1 us (54%)
  waiting for transfers between devices  26.9 us (20%)
  starting transfers between devices  19.9 us (15%)
  Pallas kernels  11.6 us (9%)
  local copies, waits for them, and re-layouts  2.48 us (2%)
    ppermute x4, waiting for transfers between devices, swap(): return lax.ppermute(x, axis, [(0, 1), (1, 0)])  26.9 us
    all_to_all x1, blocking collectives, on_device(): lanes = lax.all_to_all(lanes, ('z4', 'z2', 'z1', 'z8'), 0, 0)  22.3 us
    ppermute x4, starting transfers between devices, swap(): return lax.ppermute(x, axis, [(0, 1), (1, 0)])  19.9 us
    all_to_all x1, blocking collectives, scatter_sum(): return jnp.sum(lax.all_to_all(pieces, axes, 0, 0), axis=0)  19.3 us
    all_to_all x1, blocking collectives, gather(): lax.all_to_all(copies, axes, 0, 0).reshape(parts * x.shape[0], x.shape[1])  19.3 us
    all_to_all x1, blocking collectives, on_device(): lanes = jnp.sum(lax.all_to_all(align, ('y', 'core', 'x'), 0, 0), axis=0)  11.3 us
    pallas_call x1, Pallas kernels, precondition(): pl.pallas_call(precondition_kernel, out_shape=(jax.ShapeDtypeStruct((BLOC...  6.6 us
    pallas_call x2, Pallas kernels, gram(): pl.pallas_call(gram_kernel, out_shape=jax.ShapeDtypeStruct((SHARE, TILE),...  3.14 us
  transfers between devices with their start and end apart: 4, of which 4 were waited for; matrix products, arithmetic and copies ran while one was open for 0% of the time, Pallas kernels for 1%

profile of v2, /device:TPU:1, one launch (start us, length us, event | category | flops | bytes accessed | tf_op | source)
XLA Modules:
  0.0 133.4 jit_solution(17137942502723676541)
XLA Ops:
  0.0 1.6 %copy-done = bf16[1024,1024]{1,0:T(8,128)(2,1)S(1)} copy-done((bf16[1024,1024]{1,0:T(8,128)(2,1)S(1)}, bf16[1024,1024]{1,0:T(8,128)(2,1)}, u32[]{:S(2)}) %copy-start) | copy-done | bytes 2097176
  1.6 1.6 %gram.3 = f32[2304,128]{1,0:T(8,128)S(1)} custom-call(s32[1]{0:T(128)S(6)} %sub.3.share_ref, bf16[1024,1024]{1,0:T(8,128)(2,1)S(1)} %copy-done, bf16[1024,1024]{1,0:T(8,128)(2,1)S(1)} %copy-done), custom_call_target="tpu_custom_call" | custom-call | flops 805306368 | bytes 3145728 | tf_op jit(solution)/shard_map/gram/pallas_call | solution.py:65
  3.2 8.8 %collective-permute-start = (f32[2304,128]{1,0:T(8,128)S(1)}, f32[2304,128]{1,0:T(8,128)S(1)}, u32[]{:S(2)}, u32[]{:S(2)}) collective-permute-start(f32[2304,128]{1,0:T(8,128)S(1)} %gram.3), channel_id=1, source_target_pairs={{0,8},{8,0},{1,9},{9,1},{2,10},{10,2},{3,11},{11,3},{4,12},{12,4},... | collective-permute-start | bytes 3538952 | tf_op jit(solution)/shard_map/ppermute | solution.py:219
  12.0 1.6 %gram.2 = f32[2304,128]{1,0:T(8,128)S(1)} custom-call(s32[1]{0:T(128)} %bitcast.share_ref, bf16[1024,1024]{1,0:T(8,128)(2,1)S(1)} %copy-done.1, bf16[1024,1024]{1,0:T(8,128)(2,1)S(1)} %copy-done.1), custom_call_target="tpu_custom_call" | custom-call | flops 805306368 | bytes 3145728 | tf_op jit(solution)/shard_map/gram/pallas_call | solution.py:65
  13.6 0.9 collective-permute-done
  14.4 0.1 add.9
  14.6 19.3 %all_to_all.20 = f32[8,288,128]{2,1,0:T(8,128)S(1)} all-to-all(f32[8,288,128]{2,1,0:T(8,128)S(1)} %bitcast.7), channel_id=1, replica_groups=mesh['y'=4,'z4'=2,'z2'=2,'z1'=2,'core'=2,'x'=4,'z8'=2] {'y','z1'}, dimensions={0} | all-to-all | bytes 2359296 | tf_op jit(solution)/shard_map/all_to_all | solution.py:224
  33.8 0.1 reduce_sum.18
  33.9 1.9 %collective-permute-start.1 = (f32[288,128]{1,0:T(8,128)S(1)}, f32[288,128]{1,0:T(8,128)S(1)}, u32[]{:S(2)}, u32[]{:S(2)}) collective-permute-start(f32[288,128]{1,0:T(8,128)S(1)} %reduce_sum.18), channel_id=1, source_target_pairs={{0,32},{32,0},{1,33},{33,1},{2,34},{34,2},{3,35},{35,3},{4,36},{36... | collective-permute-start | bytes 442376 | tf_op jit(solution)/shard_map/ppermute | solution.py:219
  35.8 9.4 %collective-permute-done.1 = f32[288,128]{1,0:T(8,128)S(1)} collective-permute-done((f32[288,128]{1,0:T(8,128)S(1)}, f32[288,128]{1,0:T(8,128)S(1)}, u32[]{:S(2)}, u32[]{:S(2)}) %collective-permute-start.1) | collective-permute-done | bytes 147488 | tf_op jit(solution)/shard_map/ppermute | solution.py:219
  45.2 5.9 %collective-permute-start.2 = (f32[288,128]{1,0:T(8,128)S(1)}, f32[288,128]{1,0:T(8,128)S(1)}, u32[]{:S(2)}, u32[]{:S(2)}) collective-permute-start(f32[288,128]{1,0:T(8,128)S(1)} %add.10), channel_id=1, source_target_pairs={{0,64},{64,0},{1,65},{65,1},{2,66},{66,2},{3,67},{67,3},{4,68},{68... | collective-permute-start | bytes 442376 | tf_op jit(solution)/shard_map/ppermute | solution.py:219
  51.1 14.2 %collective-permute-done.2 = f32[288,128]{1,0:T(8,128)S(1)} collective-permute-done((f32[288,128]{1,0:T(8,128)S(1)}, f32[288,128]{1,0:T(8,128)S(1)}, u32[]{:S(2)}, u32[]{:S(2)}) %collective-permute-start.2) | collective-permute-done | bytes 147488 | tf_op jit(solution)/shard_map/ppermute | solution.py:219
  65.3 0.1 broadcast_in_dim.4
  65.4 0.0 copy-start.3
  65.4 0.0 copy-start.4
  65.4 19.3 %all_to_all.21 = f32[8,288,128]{2,1,0:T(8,128)S(1)} all-to-all(f32[8,288,128]{2,1,0:T(8,128)S(1)} %broadcast_in_dim.4), channel_id=1, replica_groups=mesh['y'=4,'z4'=2,'z2'=2,'z1'=2,'core'=2,'x'=4,'z8'=2] {'y','z1'}, dimensions={0} | all-to-all | bytes 2359296 | tf_op jit(solution)/shard_map/all_to_all | solution.py:229
  84.7 3.3 %collective-permute-start.3 = (f32[2304,128]{1,0:T(8,128)S(1)}, f32[2304,128]{1,0:T(8,128)S(1)}, u32[]{:S(2)}, u32[]{:S(2)}) collective-permute-start(f32[2304,128]{1,0:T(8,128)S(1)} %bitcast.4), channel_id=1, source_target_pairs={{0,8},{8,0},{1,9},{9,1},{2,10},{10,2},{3,11},{11,3},{4,12},{12,4},... | collective-permute-start | bytes 3538952 | tf_op jit(solution)/shard_map/ppermute | solution.py:219
  88.0 2.5 %collective-permute-done.3.other_ref = f32[2304,128]{1,0:T(8,128)S(1)} collective-permute-done((f32[2304,128]{1,0:T(8,128)S(1)}, f32[2304,128]{1,0:T(8,128)S(1)}, u32[]{:S(2)}, u32[]{:S(2)}) %collective-permute-start.3) | collective-permute-done | bytes 1179680 | tf_op jit(solution)/shard_map/ppermute | solution.py:219
  90.5 6.6 %precondition.1 = (f32[1024,128]{1,0:T(8,128)S(1)}, f32[32,1,128]{2,1,0:T(1,128)S(1)}) custom-call(s32[1]{0:T(128)} %bitcast.share_ref, f32[2304,128]{1,0:T(8,128)S(1)} %bitcast.5, f32[2304,128]{1,0:T(8,128)S(1)} %collective-permute-done.3.other_ref, bf16[1024,128]{1,0:T(8,128)(2,1)S(1)} %copy-done.3, bf16[1024,128]{1,0:T(8,128)(2,1)S(1)} %copy-done.3, ...), custom_call_target="tpu_custom_call" | custom-call | flops 2415919104 | bytes 4194304 | tf_op jit(solution)/shard_map/precondition/pallas_call | solution.py:163
  97.1 0.8 copy-done.2
  97.9 11.3 %all_to_all.22 = f32[32,1,128]{2,1,0:T(1,128)S(1)} all-to-all(f32[32,1,128]{2,1,0:T(1,128)S(1)} %get-tuple-element.8), channel_id=1, replica_groups=mesh['y'=4,'z4'=2,'z2'=2,'z1'=2,'core'=2,'x'=4,'z8'=2] {'y','core','x'}, dimensions={0} | all-to-all | bytes 32768 | tf_op jit(solution)/shard_map/all_to_all | solution.py:244
  109.2 0.1 reduce_sum.19
  109.2 22.3 %all_to_all.23.align_ref = f32[16,1,128]{2,1,0:T(1,128)} all-to-all(f32[16,1,128]{2,1,0:T(1,128)S(1)} %broadcast_in_dim.5), channel_id=1, replica_groups=mesh['y'=4,'z4'=2,'z2'=2,'z1'=2,'core'=2,'x'=4,'z8'=2] {'z4','z2','z1','..., dimensions={0} | all-to-all | bytes 16384 | tf_op jit(solution)/shard_map/all_to_all | solution.py:246
  131.5 1.9 %clip.1 = bf16[1024,128]{1,0:T(8,128)(2,1)} custom-call(f32[1024,128]{1,0:T(8,128)} %copy-done.2, f32[16,1,128]{2,1,0:T(1,128)} %all_to_all.23.align_ref), custom_call_target="tpu_custom_call" | custom-call | flops 262144 | bytes 1048576 | tf_op jit(solution)/shard_map/clip/pallas_call | solution.py:206
  (9 shorter events, 0.1 us)
Async XLA Ops:
  0.0 1.6 %copy-start = (bf16[1024,1024]{1,0:T(8,128)(2,1)S(1)}, bf16[1024,1024]{1,0:T(8,128)(2,1)}, u32[]{:S(2)}) copy-start(bf16[1024,1024]{1,0:T(8,128)(2,1)} %other_ref.3) | copy-start | bytes 6291460
  1.6 10.4 %copy-start.1 = (bf16[1024,1024]{1,0:T(8,128)(2,1)S(1)}, bf16[1024,1024]{1,0:T(8,128)(2,1)}, u32[]{:S(2)}) copy-start(bf16[1024,1024]{1,0:T(8,128)(2,1)} %other_ref.3) | copy-start | bytes 6291460
  3.2 11.3 %collective-permute-start = (f32[2304,128]{1,0:T(8,128)S(1)}, f32[2304,128]{1,0:T(8,128)S(1)}, u32[]{:S(2)}, u32[]{:S(2)}) collective-permute-start(f32[2304,128]{1,0:T(8,128)S(1)} %gram.3), channel_id=1, source_target_pairs={{0,8},{8,0},{1,9},{9,1},{2,10},{10,2},{3,11},{11,3},{4,12},{12,4},... | collective-permute-start | bytes 3538952 | tf_op jit(solution)/shard_map/ppermute | solution.py:219
  33.9 11.3 %collective-permute-start.1 = (f32[288,128]{1,0:T(8,128)S(1)}, f32[288,128]{1,0:T(8,128)S(1)}, u32[]{:S(2)}, u32[]{:S(2)}) collective-permute-start(f32[288,128]{1,0:T(8,128)S(1)} %reduce_sum.18), channel_id=1, source_target_pairs={{0,32},{32,0},{1,33},{33,1},{2,34},{34,2},{3,35},{35,3},{4,36},{36... | collective-permute-start | bytes 442376 | tf_op jit(solution)/shard_map/ppermute | solution.py:219
  45.2 20.0 %collective-permute-start.2 = (f32[288,128]{1,0:T(8,128)S(1)}, f32[288,128]{1,0:T(8,128)S(1)}, u32[]{:S(2)}, u32[]{:S(2)}) collective-permute-start(f32[288,128]{1,0:T(8,128)S(1)} %add.10), channel_id=1, source_target_pairs={{0,64},{64,0},{1,65},{65,1},{2,66},{66,2},{3,67},{67,3},{4,68},{68... | collective-permute-start | bytes 442376 | tf_op jit(solution)/shard_map/ppermute | solution.py:219
  65.4 25.1 %copy-start.3 = (bf16[1024,128]{1,0:T(8,128)(2,1)S(1)}, bf16[1024,128]{1,0:T(8,128)(2,1)}, u32[]{:S(2)}) copy-start(bf16[1024,128]{1,0:T(8,128)(2,1)} %grad_hi_ref.1) | copy-start | bytes 786436
  65.4 25.1 %copy-start.4 = (f32[128]{0:T(128)S(1)}, f32[128]{0:T(128)}, u32[]{:S(2)}) copy-start(f32[128]{0:T(128)} %param.5) | copy-start | bytes 1540
  84.7 5.8 %collective-permute-start.3 = (f32[2304,128]{1,0:T(8,128)S(1)}, f32[2304,128]{1,0:T(8,128)S(1)}, u32[]{:S(2)}, u32[]{:S(2)}) collective-permute-start(f32[2304,128]{1,0:T(8,128)S(1)} %bitcast.4), channel_id=1, source_target_pairs={{0,8},{8,0},{1,9},{9,1},{2,10},{10,2},{3,11},{11,3},{4,12},{12,4},... | collective-permute-start | bytes 3538952 | tf_op jit(solution)/shard_map/ppermute | solution.py:219
  97.1 0.8 copy-start.2

commit v3 on v2

--- a/solution.py
+++ b/solution.py
@@ -13,7 +13,8 @@
 HALF = 512
 COLS = 128
 TOKENS = 65536
-SHARE = 18 * TILE
+DIAGONALS = 16 * TILE
+SHARE = DIAGONALS + 64
 
 damping = 0.1
 kl_bound = 2.0
@@ -27,8 +28,22 @@
 bf16 = jnp.bfloat16
 
 
+def row_and_column():
+    shape = (TILE, TILE)
+    return lax.broadcasted_iota(jnp.int32, shape, 0), lax.broadcasted_iota(jnp.int32, shape, 1)
+
+
+def tile_at(ref, k):
+    return ref.at[k * TILE : (k + 1) * TILE, :]
+
+
+def off_diagonal(i, d):
+    return 2 + 3 * i + d - 1
+
+
 def gram_kernel(share_ref, own_ref, other_ref, out_ref):
     share = share_ref[0]
+    row, column = row_and_column()
 
     def product(lhs, rhs):
         return lax.dot_general(
@@ -37,6 +52,7 @@
 
     own = own_ref[...]
     other = other_ref[...]
+    out_ref[DIAGONALS:, :] = jnp.zeros((SHARE - DIAGONALS, TILE), f32)
     for pair in range(2):
         lhs = own[:, pair * 256 : (pair + 1) * 256]
         if pair == 0:
@@ -44,20 +60,22 @@
         else:
             wide = jnp.concatenate([own[:, 256:], other], axis=1)
         strip = product(lhs, wide)
+
+        def part(i, d):
+            return strip[i * TILE : (i + 1) * TILE, (i + d) * TILE : (i + d + 1) * TILE]
+
+        second = part(1, 0)
+        tile_at(out_ref, pair)[...] = jnp.where(row <= column, part(0, 0), second)
+        out_ref[DIAGONALS + pair : DIAGONALS + pair + 1, :] = jnp.sum(
+            jnp.where(row == column, second, 0.0), axis=0, keepdims=True
+        )
         for i in range(2):
-            rows = strip[i * TILE : (i + 1) * TILE]
-            for d in range(4):
-                k = (pair * 2 + i) * 4 + d
-                out_ref[k * TILE : (k + 1) * TILE, :] = rows[
-                    :, (i + d) * TILE : (i + d + 1) * TILE
-                ]
+            for d in range(1, 4):
+                tile_at(out_ref, off_diagonal(2 * pair + i, d))[...] = part(i, d)
 
             @pl.when(share == pair)
             def _():
-                k = 16 + i
-                out_ref[k * TILE : (k + 1) * TILE, :] = rows[
-                    :, (i + 4) * TILE : (i + 5) * TILE
-                ]
+                tile_at(out_ref, 14 + i)[...] = part(i, 4)
 
 
 def gram(share, activations):
@@ -91,51 +109,58 @@
     scale_ref,
     scaled_ref,
     align_ref,
-    high_ref,
-    low_ref,
+    factor_ref,
     sums_ref,
 ):
     share = share_ref[0]
-    eye = lax.broadcasted_iota(jnp.int32, (TILE, TILE), 0) == lax.broadcasted_iota(
-        jnp.int32, (TILE, TILE), 1
-    )
+    row, column = row_and_column()
     sums_ref[...] = jnp.zeros_like(sums_ref)
 
     def put(tile, i, j):
         high = tile.astype(bf16)
         low = (tile - high.astype(f32)).astype(bf16)
-        at = (slice(i * TILE, (i + 1) * TILE), slice(j * TILE, (j + 1) * TILE))
-        high_ref[at] = high
-        low_ref[at] = low
+        rows = slice(i * TILE, (i + 1) * TILE)
+        factor_ref[rows, j * TILE : (j + 1) * TILE] = high
+        factor_ref[rows, BLOCK + j * TILE : BLOCK + (j + 1) * TILE] = low
         part = jnp.abs(tile).reshape(16, 8, TILE)
         sums_ref[:, j * TILE : (j + 1) * TILE] += jnp.sum(part, axis=0)
 
     def place(ref, k, i, j):
-        tile = ref[k * TILE : (k + 1) * TILE, :] * (1.0 / TOKENS)
-        if i == j:
-            put(tile + jnp.where(eye, damping, 0.0), i, j)
-        else:
-            put(tile, i, j)
-            put(tile.T, j, i)
+        tile = tile_at(ref, k)[...] * (1.0 / TOKENS)
+        put(tile, i, j)
+        put(tile.T, j, i)
+
+    def place_diagonal(ref, pair, base):
+        tile = tile_at(ref, pair)[...] * (1.0 / TOKENS)
+        turned = tile.T
+        diagonal = ref[DIAGONALS + pair : DIAGONALS + pair + 1, :] * (1.0 / TOKENS)
+        damped = jnp.where(row == column, damping, 0.0)
+        at = base + 2 * pair
+        put(jnp.where(row <= column, tile, turned) + damped, at, at)
+        rest = jnp.where(row > column, tile, turned)
+        put(jnp.where(row == column, diagonal, rest) + damped, at + 1, at + 1)
 
     for base, ref in ((0, own_ref), (4, other_ref)):
+        for pair in range(2):
+            place_diagonal(ref, pair, base)
         for i in range(4):
-            for d in range(4):
-                place(ref, i * 4 + d, base + i, (base + i + d) % 8)
+            for d in range(1, 4):
+                place(ref, off_diagonal(i, d), base + i, (base + i + d) % 8)
     for core in range(2):
 
         @pl.when(share == core)
         def _():
             for i in range(2):
-                row = 2 * core + i
-                place(own_ref, 16 + i, row, row + 4)
-                row = 2 * (1 - core) + i
-                place(other_ref, 16 + i, row + 4, row)
+                first = 2 * core + i
+                place(own_ref, 14 + i, first, first + 4)
+                first = 2 * (1 - core) + i
+                place(other_ref, 14 + i, first + 4, first)
 
     bound = 1.0 / jnp.max(jnp.sum(sums_ref[...], axis=0, keepdims=True), axis=1, keepdims=True)
     bound2 = bound * bound
-    high = high_ref[...]
-    low = low_ref[...]
+
+    high = factor_ref[:, :BLOCK]
+    low = factor_ref[:, BLOCK:]
 
     def dot(a, b):
         return jnp.dot(a, b, preferred_element_type=f32)
@@ -143,15 +168,16 @@
     def times(v):
         v_high = v.astype(bf16)
         v_low = (v - v_high.astype(f32)).astype(bf16)
-        both = dot(high, jnp.concatenate([v_high, v_low], axis=1))
-        return both[:, :COLS] + (both[:, COLS:] + dot(low, v_high))
-
-    grad16 = jnp.concatenate([grad_lo_ref[...], grad_hi_ref[...]], axis=0)
-    grad = grad16.astype(f32)
-    u = 2.0 * bound * grad - bound2 * (dot(high, grad16) + dot(low, grad16))
+        both = dot(jnp.concatenate([v_high, v_low], axis=0), high)
+        return both[:COLS] + (both[COLS:] + dot(v_high, low))
+
+    grad = jnp.concatenate([grad_lo_ref[...], grad_hi_ref[...]], axis=0).astype(f32)
+    turned = grad.T
+    turned16 = turned.astype(bf16)
+    u = 2.0 * bound * turned - bound2 * (dot(turned16, high) + dot(turned16, low))
     v = times(u)
     applied = 2.0 * u - (2.0 * bound * v - bound2 * times(v))
-    scaled = applied * scale_ref[...]
+    scaled = applied.T * scale_ref[...]
     scaled_ref[pl.ds(pl.multiple_of(share * HALF, HALF), HALF), :] = scaled[:HALF]
     scaled_ref[pl.ds(pl.multiple_of((1 - share) * HALF, HALF), HALF), :] = scaled[HALF:]
     local = jnp.sum(scaled * grad, axis=0, keepdims=True)
@@ -181,8 +207,7 @@
                 pl.BlockSpec((copies, 1, COLS), lambda g, s: (0, 0, 0)),
             ),
             scratch_shapes=[
-                pltpu.VMEM((BLOCK, BLOCK), bf16),
-                pltpu.VMEM((BLOCK, BLOCK), bf16),
+                pltpu.VMEM((BLOCK, 2 * BLOCK), bf16),
                 pltpu.VMEM((8, BLOCK), f32),
             ],
         ),
@@ -208,6 +233,7 @@
         out_shape=jax.ShapeDtypeStruct((BLOCK, COLS), bf16),
         in_specs=[vmem, vmem],
         out_specs=vmem,
+        compiler_params=pltpu.CompilerParams(vmem_limit_bytes=4 * 2**20),
         cost_estimate=pl.CostEstimate(
             flops=2 * BLOCK * COLS, bytes_accessed=2**20, transcendentals=0
         ),

time: 134 us -> 125 us (0.933)
  waiting for transfers between devices: 26.9 us -> 22.1 us
  Pallas kernels: 11.6 us -> 7.72 us
  starting transfers between devices: 19.9 us -> 21.9 us
    ppermute x4, waiting for transfers between devices: 26.9 us -> 22.1 us  [swap(): return lax.ppermute(x, axis, [(0, 1), (1, 0)])]
    pallas_call x1, Pallas kernels: 6.6 us -> 3.73 us  [precondition(): pl.pallas_call(precondition_kernel, out_shape=(jax.ShapeDtypeStruct((BLOC...]
    ppermute x4, starting transfers between devices: 19.9 us -> 21.9 us  [swap(): return lax.ppermute(x, axis, [(0, 1), (1, 0)])]
where the time goes in v3:
time: 125 us
  blocking collectives  71.4 us (57%)
  waiting for transfers between devices  22.1 us (18%)
  starting transfers between devices  21.9 us (18%)
  Pallas kernels  7.72 us (6%)
  local copies, waits for them, and re-layouts  1.69 us (1%)
    all_to_all x1, blocking collectives, on_device(): lanes = lax.all_to_all(lanes, ('z4', 'z2', 'z1', 'z8'), 0, 0)  22.8 us
    ppermute x4, waiting for transfers between devices, swap(): return lax.ppermute(x, axis, [(0, 1), (1, 0)])  22.1 us
    ppermute x4, starting transfers between devices, swap(): return lax.ppermute(x, axis, [(0, 1), (1, 0)])  21.9 us
    all_to_all x1, blocking collectives, gather(): lax.all_to_all(copies, axes, 0, 0).reshape(parts * x.shape[0], x.shape[1])  18.9 us
    all_to_all x1, blocking collectives, scatter_sum(): return jnp.sum(lax.all_to_all(pieces, axes, 0, 0), axis=0)  18.3 us
    all_to_all x1, blocking collectives, on_device(): lanes = jnp.sum(lax.all_to_all(align, ('y', 'core', 'x'), 0, 0), axis=0)  11.4 us
    pallas_call x1, Pallas kernels, precondition(): pl.pallas_call(precondition_kernel, out_shape=(jax.ShapeDtypeStruct((BLOC...  3.73 us
    pallas_call x2, Pallas kernels, gram(): pl.pallas_call(gram_kernel, out_shape=jax.ShapeDtypeStruct((SHARE, TILE),...  3.13 us
  transfers between devices with their start and end apart: 4, of which 4 were waited for; matrix products, arithmetic and copies ran while one was open for 0% of the time, Pallas kernels for 1%

profile of v3, /device:TPU:1, one launch (start us, length us, event | category | flops | bytes accessed | tf_op | source)
XLA Modules:
  0.0 125.1 jit_solution(8500322499218188070)
XLA Ops:
  0.0 1.6 %copy-done = bf16[1024,1024]{1,0:T(8,128)(2,1)S(1)} copy-done((bf16[1024,1024]{1,0:T(8,128)(2,1)S(1)}, bf16[1024,1024]{1,0:T(8,128)(2,1)}, u32[]{:S(2)}) %copy-start) | copy-done | bytes 2097176
  1.6 1.6 %gram.3 = f32[2112,128]{1,0:T(8,128)S(1)} custom-call(s32[1]{0:T(128)S(6)} %sub.3.share_ref, bf16[1024,1024]{1,0:T(8,128)(2,1)S(1)} %copy-done, bf16[1024,1024]{1,0:T(8,128)(2,1)S(1)} %copy-done), custom_call_target="tpu_custom_call" | custom-call | flops 805306368 | bytes 3145728 | tf_op jit(solution)/shard_map/gram/pallas_call | solution.py:83
  3.2 8.8 %collective-permute-start = (f32[2112,128]{1,0:T(8,128)S(1)}, f32[2112,128]{1,0:T(8,128)S(1)}, u32[]{:S(2)}, u32[]{:S(2)}) collective-permute-start(f32[2112,128]{1,0:T(8,128)S(1)} %gram.3), channel_id=1, source_target_pairs={{0,8},{8,0},{1,9},{9,1},{2,10},{10,2},{3,11},{11,3},{4,12},{12,4},... | collective-permute-start | bytes 3244040 | tf_op jit(solution)/shard_map/ppermute | solution.py:245
  12.0 1.6 %gram.2 = f32[2112,128]{1,0:T(8,128)S(1)} custom-call(s32[1]{0:T(128)} %bitcast.share_ref, bf16[1024,1024]{1,0:T(8,128)(2,1)S(1)} %copy-done.1, bf16[1024,1024]{1,0:T(8,128)(2,1)S(1)} %copy-done.1), custom_call_target="tpu_custom_call" | custom-call | flops 805306368 | bytes 3145728 | tf_op jit(solution)/shard_map/gram/pallas_call | solution.py:83
  13.6 0.7 collective-permute-done
  14.3 0.1 add.9
  14.4 18.3 %all_to_all.20 = f32[8,264,128]{2,1,0:T(8,128)S(1)} all-to-all(f32[8,264,128]{2,1,0:T(8,128)S(1)} %bitcast.7), channel_id=1, replica_groups=mesh['y'=4,'z4'=2,'z2'=2,'z1'=2,'core'=2,'x'=4,'z8'=2] {'y','z1'}, dimensions={0} | all-to-all | bytes 2162688 | tf_op jit(solution)/shard_map/all_to_all | solution.py:250
  32.7 0.1 reduce_sum.18
  32.8 2.1 %collective-permute-start.1 = (f32[264,128]{1,0:T(8,128)S(1)}, f32[264,128]{1,0:T(8,128)S(1)}, u32[]{:S(2)}, u32[]{:S(2)}) collective-permute-start(f32[264,128]{1,0:T(8,128)S(1)} %reduce_sum.18), channel_id=1, source_target_pairs={{0,32},{32,0},{1,33},{33,1},{2,34},{34,2},{3,35},{35,3},{4,36},{36... | collective-permute-start | bytes 405512 | tf_op jit(solution)/shard_map/ppermute | solution.py:245
  34.9 8.5 %collective-permute-done.1 = f32[264,128]{1,0:T(8,128)S(1)} collective-permute-done((f32[264,128]{1,0:T(8,128)S(1)}, f32[264,128]{1,0:T(8,128)S(1)}, u32[]{:S(2)}, u32[]{:S(2)}) %collective-permute-start.1) | collective-permute-done | bytes 135200 | tf_op jit(solution)/shard_map/ppermute | solution.py:245
  43.4 7.0 %collective-permute-start.2 = (f32[264,128]{1,0:T(8,128)S(1)}, f32[264,128]{1,0:T(8,128)S(1)}, u32[]{:S(2)}, u32[]{:S(2)}) collective-permute-start(f32[264,128]{1,0:T(8,128)S(1)} %add.10), channel_id=1, source_target_pairs={{0,64},{64,0},{1,65},{65,1},{2,66},{66,2},{3,67},{67,3},{4,68},{68... | collective-permute-start | bytes 405512 | tf_op jit(solution)/shard_map/ppermute | solution.py:245
  50.4 10.5 %collective-permute-done.2 = f32[264,128]{1,0:T(8,128)S(1)} collective-permute-done((f32[264,128]{1,0:T(8,128)S(1)}, f32[264,128]{1,0:T(8,128)S(1)}, u32[]{:S(2)}, u32[]{:S(2)}) %collective-permute-start.2) | collective-permute-done | bytes 135200 | tf_op jit(solution)/shard_map/ppermute | solution.py:245
  61.0 0.1 broadcast_in_dim.4
  61.1 0.0 copy-start.2
  61.1 0.0 copy-start.3
  61.1 18.9 %all_to_all.21 = f32[8,264,128]{2,1,0:T(8,128)S(1)} all-to-all(f32[8,264,128]{2,1,0:T(8,128)S(1)} %broadcast_in_dim.4), channel_id=1, replica_groups=mesh['y'=4,'z4'=2,'z2'=2,'z1'=2,'core'=2,'x'=4,'z8'=2] {'y','z1'}, dimensions={0} | all-to-all | bytes 2162688 | tf_op jit(solution)/shard_map/all_to_all | solution.py:255
  80.0 3.9 %collective-permute-start.3 = (f32[2112,128]{1,0:T(8,128)S(1)}, f32[2112,128]{1,0:T(8,128)S(1)}, u32[]{:S(2)}, u32[]{:S(2)}) collective-permute-start(f32[2112,128]{1,0:T(8,128)S(1)} %bitcast.4), channel_id=1, source_target_pairs={{0,8},{8,0},{1,9},{9,1},{2,10},{10,2},{3,11},{11,3},{4,12},{12,4},... | collective-permute-start | bytes 3244040 | tf_op jit(solution)/shard_map/ppermute | solution.py:245
  83.9 2.3 %collective-permute-done.3.other_ref = f32[2112,128]{1,0:T(8,128)S(1)} collective-permute-done((f32[2112,128]{1,0:T(8,128)S(1)}, f32[2112,128]{1,0:T(8,128)S(1)}, u32[]{:S(2)}, u32[]{:S(2)}) %collective-permute-start.3) | collective-permute-done | bytes 1081376 | tf_op jit(solution)/shard_map/ppermute | solution.py:245
  86.2 0.0 copy-done.3
  86.2 3.7 %precondition.1 = (f32[1024,128]{1,0:T(8,128)S(1)}, f32[32,1,128]{2,1,0:T(1,128)S(1)}) custom-call(s32[1]{0:T(128)} %bitcast.share_ref, f32[2112,128]{1,0:T(8,128)S(1)} %bitcast.5, f32[2112,128]{1,0:T(8,128)S(1)} %collective-permute-done.3.other_ref, bf16[1024,128]{1,0:T(8,128)(2,1)S(1)} %copy-done.2, bf16[1024,128]{1,0:T(8,128)(2,1)S(1)} %copy-done.2, ...), custom_call_target="tpu_custom_call" | custom-call | flops 2415919104 | bytes 4194304 | tf_op jit(solution)/shard_map/precondition/pallas_call | solution.py:189
  90.0 11.4 %all_to_all.22 = f32[32,1,128]{2,1,0:T(1,128)S(1)} all-to-all(f32[32,1,128]{2,1,0:T(1,128)S(1)} %get-tuple-element.8), channel_id=1, replica_groups=mesh['y'=4,'z4'=2,'z2'=2,'z1'=2,'core'=2,'x'=4,'z8'=2] {'y','core','x'}, dimensions={0} | all-to-all | bytes 32768 | tf_op jit(solution)/shard_map/all_to_all | solution.py:270
  101.3 0.1 reduce_sum.19
  101.4 22.8 %all_to_all.23.align_ref = f32[16,1,128]{2,1,0:T(1,128)S(1)} all-to-all(f32[16,1,128]{2,1,0:T(1,128)S(1)} %broadcast_in_dim.5), channel_id=1, replica_groups=mesh['y'=4,'z4'=2,'z2'=2,'z1'=2,'core'=2,'x'=4,'z8'=2] {'z4','z2','z1','..., dimensions={0} | all-to-all | bytes 16384 | tf_op jit(solution)/shard_map/all_to_all | solution.py:272
  124.2 0.9 clip.1
  (7 shorter events, 0.1 us)
Async XLA Ops:
  0.0 1.6 %copy-start = (bf16[1024,1024]{1,0:T(8,128)(2,1)S(1)}, bf16[1024,1024]{1,0:T(8,128)(2,1)}, u32[]{:S(2)}) copy-start(bf16[1024,1024]{1,0:T(8,128)(2,1)} %other_ref.3) | copy-start | bytes 6291460
  1.6 10.4 %copy-start.1 = (bf16[1024,1024]{1,0:T(8,128)(2,1)S(1)}, bf16[1024,1024]{1,0:T(8,128)(2,1)}, u32[]{:S(2)}) copy-start(bf16[1024,1024]{1,0:T(8,128)(2,1)} %other_ref.3) | copy-start | bytes 6291460
  3.2 11.1 %collective-permute-start = (f32[2112,128]{1,0:T(8,128)S(1)}, f32[2112,128]{1,0:T(8,128)S(1)}, u32[]{:S(2)}, u32[]{:S(2)}) collective-permute-start(f32[2112,128]{1,0:T(8,128)S(1)} %gram.3), channel_id=1, source_target_pairs={{0,8},{8,0},{1,9},{9,1},{2,10},{10,2},{3,11},{11,3},{4,12},{12,4},... | collective-permute-start | bytes 3244040 | tf_op jit(solution)/shard_map/ppermute | solution.py:245
  32.8 10.7 %collective-permute-start.1 = (f32[264,128]{1,0:T(8,128)S(1)}, f32[264,128]{1,0:T(8,128)S(1)}, u32[]{:S(2)}, u32[]{:S(2)}) collective-permute-start(f32[264,128]{1,0:T(8,128)S(1)} %reduce_sum.18), channel_id=1, source_target_pairs={{0,32},{32,0},{1,33},{33,1},{2,34},{34,2},{3,35},{35,3},{4,36},{36... | collective-permute-start | bytes 405512 | tf_op jit(solution)/shard_map/ppermute | solution.py:245
  43.4 17.5 %collective-permute-start.2 = (f32[264,128]{1,0:T(8,128)S(1)}, f32[264,128]{1,0:T(8,128)S(1)}, u32[]{:S(2)}, u32[]{:S(2)}) collective-permute-start(f32[264,128]{1,0:T(8,128)S(1)} %add.10), channel_id=1, source_target_pairs={{0,64},{64,0},{1,65},{65,1},{2,66},{66,2},{3,67},{67,3},{4,68},{68... | collective-permute-start | bytes 405512 | tf_op jit(solution)/shard_map/ppermute | solution.py:245
  61.1 25.2 %copy-start.2 = (bf16[1024,128]{1,0:T(8,128)(2,1)S(1)}, bf16[1024,128]{1,0:T(8,128)(2,1)}, u32[]{:S(2)}) copy-start(bf16[1024,128]{1,0:T(8,128)(2,1)} %grad_hi_ref.1) | copy-start | bytes 786436
  61.1 25.1 %copy-start.3 = (f32[128]{0:T(128)S(1)}, f32[128]{0:T(128)}, u32[]{:S(2)}) copy-start(f32[128]{0:T(128)} %param.5) | copy-start | bytes 1540
  80.0 6.2 %collective-permute-start.3 = (f32[2112,128]{1,0:T(8,128)S(1)}, f32[2112,128]{1,0:T(8,128)S(1)}, u32[]{:S(2)}, u32[]{:S(2)}) collective-permute-start(f32[2112,128]{1,0:T(8,128)S(1)} %bitcast.4), channel_id=1, source_target_pairs={{0,8},{8,0},{1,9},{9,1},{2,10},{10,2},{3,11},{11,3},{4,12},{12,4},... | collective-permute-start | bytes 3244040 | tf_op jit(solution)/shard_map/ppermute | solution.py:245

commit v4 on v3

--- a/solution.py
+++ b/solution.py
@@ -245,6 +245,18 @@
     return lax.ppermute(x, axis, [(0, 1), (1, 0)])
 
 
+def cross(x, order):
+    pairs = []
+    for rank in range(16):
+        z4, z2, z1, core = rank >> 3, (rank >> 2) & 1, (rank >> 1) & 1, rank & 1
+        if core == order:
+            z2 = 1 - z2
+        else:
+            z4 = 1 - z4
+        pairs.append((rank, z4 * 8 + z2 * 4 + z1 * 2 + core))
+    return lax.ppermute(x, ("z4", "z2", "z1", "core"), pairs)
+
+
 def scatter_sum(x, axes, parts):
     pieces = x.reshape(parts, x.shape[0] // parts, x.shape[1])
     return jnp.sum(lax.all_to_all(pieces, axes, 0, 0), axis=0)
@@ -262,8 +274,8 @@
     away = swap(gram(theirs, activations), "core")
     chip = gram(mine, activations) + away
     part = scatter_sum(chip, ("y", "z1"), 8)
-    part = part + swap(part, "z2")
-    part = part + swap(part, "z4")
+    part = part + cross(part, 0)
+    part = part + cross(part, 1)
     own = gather(part, ("y", "z1"), 8)
     other = swap(own, "core")
     scaled, align = precondition(mine, own, other, gradient, out_scale, 32)

time: 125 us -> 118 us (0.944)
  waiting for transfers between devices: 22.1 us -> 15.7 us
  blocking collectives: 71.4 us -> 67.6 us
  starting transfers between devices: 21.9 us -> 24.8 us
    ppermute x4 -> x2, waiting for transfers between devices: 22.1 us -> 3.04 us  [swap(): return lax.ppermute(x, axis, [(0, 1), (1, 0)])]
    ppermute x0 -> x2, waiting for transfers between devices: none -> 12.7 us  [cross(): return lax.ppermute(x, ('z4', 'z2', 'z1', 'core'), pairs)]
    ppermute x0 -> x2, starting transfers between devices: none -> 10.6 us  [cross(): return lax.ppermute(x, ('z4', 'z2', 'z1', 'core'), pairs)]
    ppermute x4 -> x2, starting transfers between devices: 21.9 us -> 14.2 us  [swap(): return lax.ppermute(x, axis, [(0, 1), (1, 0)])]
    all_to_all x1, blocking collectives: 18.9 us -> 16.2 us  [gather(): lax.all_to_all(copies, axes, 0, 0).reshape(parts * x.shape[0], x.shape[1])]
    all_to_all x1, blocking collectives: 22.8 us -> 20.3 us  [on_device(): lanes = lax.all_to_all(lanes, ('z4', 'z2', 'z1', 'z8'), 0, 0)]
    all_to_all x1, blocking collectives: 11.4 us -> 12.8 us  [on_device(): lanes = jnp.sum(lax.all_to_all(align, ('y', 'core', 'x'), 0, 0), axis=0)]
where the time goes in v4:
time: 118 us
  blocking collectives  67.6 us (57%)
  starting transfers between devices  24.8 us (21%)
  waiting for transfers between devices  15.7 us (13%)
  Pallas kernels  7.72 us (7%)
  local copies, waits for them, and re-layouts  1.69 us (1%)
    all_to_all x1, blocking collectives, on_device(): lanes = lax.all_to_all(lanes, ('z4', 'z2', 'z1', 'z8'), 0, 0)  20.3 us
    all_to_all x1, blocking collectives, scatter_sum(): return jnp.sum(lax.all_to_all(pieces, axes, 0, 0), axis=0)  18.3 us
    all_to_all x1, blocking collectives, gather(): lax.all_to_all(copies, axes, 0, 0).reshape(parts * x.shape[0], x.shape[1])  16.2 us
    ppermute x2, starting transfers between devices, swap(): return lax.ppermute(x, axis, [(0, 1), (1, 0)])  14.2 us
    all_to_all x1, blocking collectives, on_device(): lanes = jnp.sum(lax.all_to_all(align, ('y', 'core', 'x'), 0, 0), axis=0)  12.8 us
    ppermute x2, waiting for transfers between devices, cross(): return lax.ppermute(x, ('z4', 'z2', 'z1', 'core'), pairs)  12.7 us
    ppermute x2, starting transfers between devices, cross(): return lax.ppermute(x, ('z4', 'z2', 'z1', 'core'), pairs)  10.6 us
    pallas_call x1, Pallas kernels, precondition(): pl.pallas_call(precondition_kernel, out_shape=(jax.ShapeDtypeStruct((BLOC...  3.73 us
  transfers between devices with their start and end apart: 4, of which 4 were waited for; matrix products, arithmetic and copies ran while one was open for 0% of the time, Pallas kernels for 1%

profile of v4, /device:TPU:1, one launch (start us, length us, event | category | flops | bytes accessed | tf_op | source)
XLA Modules:
  0.0 117.9 jit_solution(15569745472471443573)
XLA Ops:
  0.0 1.6 %copy-done = bf16[1024,1024]{1,0:T(8,128)(2,1)S(1)} copy-done((bf16[1024,1024]{1,0:T(8,128)(2,1)S(1)}, bf16[1024,1024]{1,0:T(8,128)(2,1)}, u32[]{:S(2)}) %copy-start) | copy-done | bytes 2097176
  1.6 1.6 %gram.3 = f32[2112,128]{1,0:T(8,128)S(1)} custom-call(s32[1]{0:T(128)S(6)} %sub.3.share_ref, bf16[1024,1024]{1,0:T(8,128)(2,1)S(1)} %copy-done, bf16[1024,1024]{1,0:T(8,128)(2,1)S(1)} %copy-done), custom_call_target="tpu_custom_call" | custom-call | flops 805306368 | bytes 3145728 | tf_op jit(solution)/shard_map/gram/pallas_call | solution.py:83
  3.2 8.8 %collective-permute-start = (f32[2112,128]{1,0:T(8,128)S(1)}, f32[2112,128]{1,0:T(8,128)S(1)}, u32[]{:S(2)}, u32[]{:S(2)}) collective-permute-start(f32[2112,128]{1,0:T(8,128)S(1)} %gram.3), channel_id=1, source_target_pairs={{0,8},{8,0},{1,9},{9,1},{2,10},{10,2},{3,11},{11,3},{4,12},{12,4},... | collective-permute-start | bytes 3244040 | tf_op jit(solution)/shard_map/ppermute | solution.py:245
  12.0 0.0 copy-done.1
  12.0 1.6 %gram.2 = f32[2112,128]{1,0:T(8,128)S(1)} custom-call(s32[1]{0:T(128)} %bitcast.share_ref, bf16[1024,1024]{1,0:T(8,128)(2,1)S(1)} %copy-done.1, bf16[1024,1024]{1,0:T(8,128)(2,1)S(1)} %copy-done.1), custom_call_target="tpu_custom_call" | custom-call | flops 805306368 | bytes 3145728 | tf_op jit(solution)/shard_map/gram/pallas_call | solution.py:83
  13.6 0.7 collective-permute-done
  14.3 0.1 add.9
  14.4 18.3 %all_to_all.20 = f32[8,264,128]{2,1,0:T(8,128)S(1)} all-to-all(f32[8,264,128]{2,1,0:T(8,128)S(1)} %bitcast.7), channel_id=1, replica_groups=mesh['y'=4,'z4'=2,'z2'=2,'z1'=2,'core'=2,'x'=4,'z8'=2] {'y','z1'}, dimensions={0} | all-to-all | bytes 2162688 | tf_op jit(solution)/shard_map/all_to_all | solution.py:262
  32.7 0.1 reduce_sum.18
  32.8 6.1 %collective-permute-start.1 = (f32[264,128]{1,0:T(8,128)S(1)}, f32[264,128]{1,0:T(8,128)S(1)}, u32[]{:S(2)}, u32[]{:S(2)}) collective-permute-start(f32[264,128]{1,0:T(8,128)S(1)} %reduce_sum.18), channel_id=1, source_target_pairs={{0,32},{8,72},{16,48},{24,88},{32,0},{40,104},{48,16},{56,120},{64... | collective-permute-start | bytes 405512 | tf_op jit(solution)/shard_map/ppermute | solution.py:257
  38.8 6.8 %collective-permute-done.1 = f32[264,128]{1,0:T(8,128)S(1)} collective-permute-done((f32[264,128]{1,0:T(8,128)S(1)}, f32[264,128]{1,0:T(8,128)S(1)}, u32[]{:S(2)}, u32[]{:S(2)}) %collective-permute-start.1) | collective-permute-done | bytes 135200 | tf_op jit(solution)/shard_map/ppermute | solution.py:257
  45.7 4.5 %collective-permute-start.2 = (f32[264,128]{1,0:T(8,128)S(1)}, f32[264,128]{1,0:T(8,128)S(1)}, u32[]{:S(2)}, u32[]{:S(2)}) collective-permute-start(f32[264,128]{1,0:T(8,128)S(1)} %add.10), channel_id=1, source_target_pairs={{0,64},{8,40},{16,80},{24,56},{32,96},{40,8},{48,112},{56,24},{64,... | collective-permute-start | bytes 405512 | tf_op jit(solution)/shard_map/ppermute | solution.py:257
  50.2 5.8 %collective-permute-done.2 = f32[264,128]{1,0:T(8,128)S(1)} collective-permute-done((f32[264,128]{1,0:T(8,128)S(1)}, f32[264,128]{1,0:T(8,128)S(1)}, u32[]{:S(2)}, u32[]{:S(2)}) %collective-permute-start.2) | collective-permute-done | bytes 135200 | tf_op jit(solution)/shard_map/ppermute | solution.py:257
  56.1 0.1 broadcast_in_dim.4
  56.2 0.0 copy-start.2
  56.2 0.0 copy-start.3
  56.2 16.2 %all_to_all.21 = f32[8,264,128]{2,1,0:T(8,128)S(1)} all-to-all(f32[8,264,128]{2,1,0:T(8,128)S(1)} %broadcast_in_dim.4), channel_id=1, replica_groups=mesh['y'=4,'z4'=2,'z2'=2,'z1'=2,'core'=2,'x'=4,'z8'=2] {'y','z1'}, dimensions={0} | all-to-all | bytes 2162688 | tf_op jit(solution)/shard_map/all_to_all | solution.py:267
  72.4 5.4 %collective-permute-start.3 = (f32[2112,128]{1,0:T(8,128)S(1)}, f32[2112,128]{1,0:T(8,128)S(1)}, u32[]{:S(2)}, u32[]{:S(2)}) collective-permute-start(f32[2112,128]{1,0:T(8,128)S(1)} %bitcast.4), channel_id=1, source_target_pairs={{0,8},{8,0},{1,9},{9,1},{2,10},{10,2},{3,11},{11,3},{4,12},{12,4},... | collective-permute-start | bytes 3244040 | tf_op jit(solution)/shard_map/ppermute | solution.py:245
  77.8 2.3 %collective-permute-done.3.other_ref = f32[2112,128]{1,0:T(8,128)S(1)} collective-permute-done((f32[2112,128]{1,0:T(8,128)S(1)}, f32[2112,128]{1,0:T(8,128)S(1)}, u32[]{:S(2)}, u32[]{:S(2)}) %collective-permute-start.3) | collective-permute-done | bytes 1081376 | tf_op jit(solution)/shard_map/ppermute | solution.py:245
  80.2 3.7 %precondition.1 = (f32[1024,128]{1,0:T(8,128)S(1)}, f32[32,1,128]{2,1,0:T(1,128)S(1)}) custom-call(s32[1]{0:T(128)} %bitcast.share_ref, f32[2112,128]{1,0:T(8,128)S(1)} %bitcast.5, f32[2112,128]{1,0:T(8,128)S(1)} %collective-permute-done.3.other_ref, bf16[1024,128]{1,0:T(8,128)(2,1)S(1)} %copy-done.2, bf16[1024,128]{1,0:T(8,128)(2,1)S(1)} %copy-done.2, ...), custom_call_target="tpu_custom_call" | custom-call | flops 2415919104 | bytes 4194304 | tf_op jit(solution)/shard_map/precondition/pallas_call | solution.py:189
  83.9 12.8 %all_to_all.22 = f32[32,1,128]{2,1,0:T(1,128)S(1)} all-to-all(f32[32,1,128]{2,1,0:T(1,128)S(1)} %get-tuple-element.8), channel_id=1, replica_groups=mesh['y'=4,'z4'=2,'z2'=2,'z1'=2,'core'=2,'x'=4,'z8'=2] {'y','core','x'}, dimensions={0} | all-to-all | bytes 32768 | tf_op jit(solution)/shard_map/all_to_all | solution.py:282
  96.7 0.1 reduce_sum.19
  96.7 20.3 %all_to_all.23.align_ref = f32[16,1,128]{2,1,0:T(1,128)S(1)} all-to-all(f32[16,1,128]{2,1,0:T(1,128)S(1)} %broadcast_in_dim.5), channel_id=1, replica_groups=mesh['y'=4,'z4'=2,'z2'=2,'z1'=2,'core'=2,'x'=4,'z8'=2] {'z4','z2','z1','..., dimensions={0} | all-to-all | bytes 16384 | tf_op jit(solution)/shard_map/all_to_all | solution.py:284
  117.0 0.9 clip.1
  (7 shorter events, 0.1 us)
Async XLA Ops:
  0.0 1.6 %copy-start = (bf16[1024,1024]{1,0:T(8,128)(2,1)S(1)}, bf16[1024,1024]{1,0:T(8,128)(2,1)}, u32[]{:S(2)}) copy-start(bf16[1024,1024]{1,0:T(8,128)(2,1)} %other_ref.3) | copy-start | bytes 6291460
  1.6 10.4 %copy-start.1 = (bf16[1024,1024]{1,0:T(8,128)(2,1)S(1)}, bf16[1024,1024]{1,0:T(8,128)(2,1)}, u32[]{:S(2)}) copy-start(bf16[1024,1024]{1,0:T(8,128)(2,1)} %other_ref.3) | copy-start | bytes 6291460
  3.2 11.1 %collective-permute-start = (f32[2112,128]{1,0:T(8,128)S(1)}, f32[2112,128]{1,0:T(8,128)S(1)}, u32[]{:S(2)}, u32[]{:S(2)}) collective-permute-start(f32[2112,128]{1,0:T(8,128)S(1)} %gram.3), channel_id=1, source_target_pairs={{0,8},{8,0},{1,9},{9,1},{2,10},{10,2},{3,11},{11,3},{4,12},{12,4},... | collective-permute-start | bytes 3244040 | tf_op jit(solution)/shard_map/ppermute | solution.py:245
  32.8 12.9 %collective-permute-start.1 = (f32[264,128]{1,0:T(8,128)S(1)}, f32[264,128]{1,0:T(8,128)S(1)}, u32[]{:S(2)}, u32[]{:S(2)}) collective-permute-start(f32[264,128]{1,0:T(8,128)S(1)} %reduce_sum.18), channel_id=1, source_target_pairs={{0,32},{8,72},{16,48},{24,88},{32,0},{40,104},{48,16},{56,120},{64... | collective-permute-start | bytes 405512 | tf_op jit(solution)/shard_map/ppermute | solution.py:257
  45.7 10.4 %collective-permute-start.2 = (f32[264,128]{1,0:T(8,128)S(1)}, f32[264,128]{1,0:T(8,128)S(1)}, u32[]{:S(2)}, u32[]{:S(2)}) collective-permute-start(f32[264,128]{1,0:T(8,128)S(1)} %add.10), channel_id=1, source_target_pairs={{0,64},{8,40},{16,80},{24,56},{32,96},{40,8},{48,112},{56,24},{64,... | collective-permute-start | bytes 405512 | tf_op jit(solution)/shard_map/ppermute | solution.py:257
  56.2 24.0 %copy-start.2 = (bf16[1024,128]{1,0:T(8,128)(2,1)S(1)}, bf16[1024,128]{1,0:T(8,128)(2,1)}, u32[]{:S(2)}) copy-start(bf16[1024,128]{1,0:T(8,128)(2,1)} %grad_hi_ref.1) | copy-start | bytes 786436
  56.2 24.0 %copy-start.3 = (f32[128]{0:T(128)S(1)}, f32[128]{0:T(128)}, u32[]{:S(2)}) copy-start(f32[128]{0:T(128)} %param.5) | copy-start | bytes 1540
  72.4 7.7 %collective-permute-start.3 = (f32[2112,128]{1,0:T(8,128)S(1)}, f32[2112,128]{1,0:T(8,128)S(1)}, u32[]{:S(2)}, u32[]{:S(2)}) collective-permute-start(f32[2112,128]{1,0:T(8,128)S(1)} %bitcast.4), channel_id=1, source_target_pairs={{0,8},{8,0},{1,9},{9,1},{2,10},{10,2},{3,11},{11,3},{4,12},{12,4},... | collective-permute-start | bytes 3244040 | tf_op jit(solution)/shard_map/ppermute | solution.py:245

commit v5 on v4

--- a/solution.py
+++ b/solution.py
@@ -100,61 +100,93 @@
     )(share, activations, activations)
 
 
+def put(factor_ref, sums_ref, tile, i, j):
+    high = tile.astype(bf16)
+    low = (tile - high.astype(f32)).astype(bf16)
+    rows = slice(i * TILE, (i + 1) * TILE)
+    factor_ref[rows, j * TILE : (j + 1) * TILE] = high
+    factor_ref[rows, BLOCK + j * TILE : BLOCK + (j + 1) * TILE] = low
+    part = jnp.abs(tile).reshape(16, 8, TILE)
+    sums_ref[:, j * TILE : (j + 1) * TILE] += jnp.sum(part, axis=0)
+
+
+def unpack(share_ref, packed_ref, factor_ref, sums_ref, base):
+    share = share_ref[0]
+    row, column = row_and_column()
+
+    def place(k, i, j):
+        tile = tile_at(packed_ref, k)[...] * (1.0 / TOKENS)
+        put(factor_ref, sums_ref, tile, i, j)
+        put(factor_ref, sums_ref, tile.T, j, i)
+
+    def place_diagonal(pair):
+        tile = tile_at(packed_ref, pair)[...] * (1.0 / TOKENS)
+        turned = tile.T
+        diagonal = packed_ref[DIAGONALS + pair : DIAGONALS + pair + 1, :] * (1.0 / TOKENS)
+        damped = jnp.where(row == column, damping, 0.0)
+        at = base + 2 * pair
+        first = jnp.where(row <= column, tile, turned) + damped
+        put(factor_ref, sums_ref, first, at, at)
+        rest = jnp.where(row > column, tile, turned)
+        second = jnp.where(row == column, diagonal, rest) + damped
+        put(factor_ref, sums_ref, second, at + 1, at + 1)
+
+    for pair in range(2):
+        place_diagonal(pair)
+    for i in range(4):
+        for d in range(1, 4):
+            place(off_diagonal(i, d), base + i, (base + i + d) % 8)
+    for core in range(2):
+
+        @pl.when(share == core)
+        def _():
+            owner = core if base == 0 else 1 - core
+            for i in range(2):
+                first = base + 2 * owner + i
+                place(14 + i, first, (first + 4) % 8)
+
+
+def unpack_kernel(share_ref, own_ref, factor_ref, sums_ref):
+    sums_ref[...] = jnp.zeros_like(sums_ref)
+    unpack(share_ref, own_ref, factor_ref, sums_ref, 0)
+
+
+def unpack_own(share, own):
+    vmem = pl.BlockSpec(memory_space=pltpu.VMEM)
+    return pl.pallas_call(
+        unpack_kernel,
+        out_shape=(
+            jax.ShapeDtypeStruct((BLOCK, 2 * BLOCK), bf16),
+            jax.ShapeDtypeStruct((8, BLOCK), f32),
+        ),
+        in_specs=[pl.BlockSpec(memory_space=pltpu.SMEM), vmem],
+        out_specs=(vmem, vmem),
+        compiler_params=pltpu.CompilerParams(vmem_limit_bytes=16 * 2**20),
+        cost_estimate=pl.CostEstimate(
+            flops=2 * BLOCK * BLOCK, bytes_accessed=5 * 2**20, transcendentals=0
+        ),
+        name="unpack_own",
+    )(share, own)
+
+
 def precondition_kernel(
     share_ref,
-    own_ref,
+    half_factor_ref,
+    own_sums_ref,
     other_ref,
-    grad_lo_ref,
-    grad_hi_ref,
+    grad_ref,
     scale_ref,
+    factor_ref,
     scaled_ref,
     align_ref,
-    factor_ref,
     sums_ref,
 ):
+    del half_factor_ref
     share = share_ref[0]
-    row, column = row_and_column()
-    sums_ref[...] = jnp.zeros_like(sums_ref)
-
-    def put(tile, i, j):
-        high = tile.astype(bf16)
-        low = (tile - high.astype(f32)).astype(bf16)
-        rows = slice(i * TILE, (i + 1) * TILE)
-        factor_ref[rows, j * TILE : (j + 1) * TILE] = high
-        factor_ref[rows, BLOCK + j * TILE : BLOCK + (j + 1) * TILE] = low
-        part = jnp.abs(tile).reshape(16, 8, TILE)
-        sums_ref[:, j * TILE : (j + 1) * TILE] += jnp.sum(part, axis=0)
-
-    def place(ref, k, i, j):
-        tile = tile_at(ref, k)[...] * (1.0 / TOKENS)
-        put(tile, i, j)
-        put(tile.T, j, i)
-
-    def place_diagonal(ref, pair, base):
-        tile = tile_at(ref, pair)[...] * (1.0 / TOKENS)
-        turned = tile.T
-        diagonal = ref[DIAGONALS + pair : DIAGONALS + pair + 1, :] * (1.0 / TOKENS)
-        damped = jnp.where(row == column, damping, 0.0)
-        at = base + 2 * pair
-        put(jnp.where(row <= column, tile, turned) + damped, at, at)
-        rest = jnp.where(row > column, tile, turned)
-        put(jnp.where(row == column, diagonal, rest) + damped, at + 1, at + 1)
-
-    for base, ref in ((0, own_ref), (4, other_ref)):
-        for pair in range(2):
-            place_diagonal(ref, pair, base)
-        for i in range(4):
-            for d in range(1, 4):
-                place(ref, off_diagonal(i, d), base + i, (base + i + d) % 8)
-    for core in range(2):
-
-        @pl.when(share == core)
-        def _():
-            for i in range(2):
-                first = 2 * core + i
-                place(own_ref, 14 + i, first, first + 4)
-                first = 2 * (1 - core) + i
-                place(other_ref, 14 + i, first + 4, first)
+    own_rows = pl.ds(pl.multiple_of(share * HALF, HALF), HALF)
+    other_rows = pl.ds(pl.multiple_of((1 - share) * HALF, HALF), HALF)
+    sums_ref[...] = own_sums_ref[...]
+    unpack(share_ref, other_ref, factor_ref, sums_ref, 4)
 
     bound = 1.0 / jnp.max(jnp.sum(sums_ref[...], axis=0, keepdims=True), axis=1, keepdims=True)
     bound2 = bound * bound
@@ -171,52 +203,39 @@
         both = dot(jnp.concatenate([v_high, v_low], axis=0), high)
         return both[:COLS] + (both[COLS:] + dot(v_high, low))
 
-    grad = jnp.concatenate([grad_lo_ref[...], grad_hi_ref[...]], axis=0).astype(f32)
+    grad = jnp.concatenate([grad_ref[own_rows, :], grad_ref[other_rows, :]], axis=0).astype(f32)
     turned = grad.T
     turned16 = turned.astype(bf16)
     u = 2.0 * bound * turned - bound2 * (dot(turned16, high) + dot(turned16, low))
     v = times(u)
     applied = 2.0 * u - (2.0 * bound * v - bound2 * times(v))
     scaled = applied.T * scale_ref[...]
-    scaled_ref[pl.ds(pl.multiple_of(share * HALF, HALF), HALF), :] = scaled[:HALF]
-    scaled_ref[pl.ds(pl.multiple_of((1 - share) * HALF, HALF), HALF), :] = scaled[HALF:]
+    scaled_ref[own_rows, :] = scaled[:HALF]
+    scaled_ref[other_rows, :] = scaled[HALF:]
     local = jnp.sum(scaled * grad, axis=0, keepdims=True)
     align_ref[...] = jnp.broadcast_to(local[None], align_ref.shape)
 
 
-def precondition(share, own, other, gradient, out_scale, copies):
-    whole = lambda g, s: (0, 0)
-    return pl.pallas_call(
+def precondition(share, half_factor, own_sums, other, gradient, out_scale, copies):
+    vmem = pl.BlockSpec(memory_space=pltpu.VMEM)
+    outputs = pl.pallas_call(
         precondition_kernel,
         out_shape=(
+            jax.ShapeDtypeStruct((BLOCK, 2 * BLOCK), bf16),
             jax.ShapeDtypeStruct((BLOCK, COLS), f32),
             jax.ShapeDtypeStruct((copies, 1, COLS), f32),
         ),
-        grid_spec=pltpu.PrefetchScalarGridSpec(
-            num_scalar_prefetch=1,
-            grid=(1,),
-            in_specs=[
-                pl.BlockSpec((SHARE, TILE), whole),
-                pl.BlockSpec((SHARE, TILE), whole),
-                pl.BlockSpec((HALF, COLS), lambda g, s: (s[0], 0)),
-                pl.BlockSpec((HALF, COLS), lambda g, s: (1 - s[0], 0)),
-                pl.BlockSpec((1, COLS), whole),
-            ],
-            out_specs=(
-                pl.BlockSpec((BLOCK, COLS), whole),
-                pl.BlockSpec((copies, 1, COLS), lambda g, s: (0, 0, 0)),
-            ),
-            scratch_shapes=[
-                pltpu.VMEM((BLOCK, 2 * BLOCK), bf16),
-                pltpu.VMEM((8, BLOCK), f32),
-            ],
-        ),
-        compiler_params=pltpu.CompilerParams(vmem_limit_bytes=40 * 2**20),
+        in_specs=[pl.BlockSpec(memory_space=pltpu.SMEM)] + [vmem] * 5,
+        out_specs=(vmem, vmem, vmem),
+        scratch_shapes=[pltpu.VMEM((8, BLOCK), f32)],
+        input_output_aliases={1: 0},
+        compiler_params=pltpu.CompilerParams(vmem_limit_bytes=24 * 2**20),
         cost_estimate=pl.CostEstimate(
             flops=2 * 9 * BLOCK * BLOCK * COLS, bytes_accessed=4 * 2**20, transcendentals=0
         ),
         name="precondition",
-    )(share, own, other, gradient, gradient, out_scale.reshape(1, COLS))
+    )(share, half_factor, own_sums, other, gradient, out_scale.reshape(1, COLS))
+    return outputs[1:]
 
 
 def clip_kernel(scaled_ref, align_ref, out_ref):
@@ -273,12 +292,13 @@
     theirs = 1 - mine
     away = swap(gram(theirs, activations), "core")
     chip = gram(mine, activations) + away
-    part = scatter_sum(chip, ("y", "z1"), 8)
+    part = scatter_sum(chip, ("z1", "y"), 8)
     part = part + cross(part, 0)
     part = part + cross(part, 1)
-    own = gather(part, ("y", "z1"), 8)
+    own = gather(part, ("z1", "y"), 8)
     other = swap(own, "core")
-    scaled, align = precondition(mine, own, other, gradient, out_scale, 32)
+    half_factor, own_sums = unpack_own(mine, own)
+    scaled, align = precondition(mine, half_factor, own_sums, other, gradient, out_scale, 32)
     lanes = jnp.sum(lax.all_to_all(align, ("y", "core", "x"), 0, 0), axis=0)
     lanes = jnp.broadcast_to(lanes[None], (16, 1, COLS))
     lanes = lax.all_to_all(lanes, ("z4", "z2", "z1", "z8"), 0, 0)

time: 118 us -> 118 us (level)
  transfers between devices with their start and end apart: 4 -> 4, of which waited for: 4 -> 4; matrix products, arithmetic and copies ran while one was open for 0% -> 0% of each run, Pallas kernels for 1% -> 2%
where the time goes in v5:
time: 118 us; the launch traced here: 117 us
  blocking collectives  67.3 us (57%)
  starting transfers between devices  24.6 us (21%)
  waiting for transfers between devices  15.3 us (13%)
  Pallas kernels  7.85 us (7%)
  local copies, waits for them, and re-layouts  1.68 us (1%)
    all_to_all x1, blocking collectives, on_device(): lanes = lax.all_to_all(lanes, ('z4', 'z2', 'z1', 'z8'), 0, 0)  20.3 us
    all_to_all x1, blocking collectives, scatter_sum(): return jnp.sum(lax.all_to_all(pieces, axes, 0, 0), axis=0)  18.3 us
    all_to_all x1, blocking collectives, gather(): lax.all_to_all(copies, axes, 0, 0).reshape(parts * x.shape[0], x.shape[1])  16.3 us
    ppermute x2, starting transfers between devices, swap(): return lax.ppermute(x, axis, [(0, 1), (1, 0)])  14.2 us
    ppermute x2, waiting for transfers between devices, cross(): return lax.ppermute(x, ('z4', 'z2', 'z1', 'core'), pairs)  12.9 us
    all_to_all x1, blocking collectives, on_device(): lanes = jnp.sum(lax.all_to_all(align, ('y', 'core', 'x'), 0, 0), axis=0)  12.4 us
    ppermute x2, starting transfers between devices, cross(): return lax.ppermute(x, ('z4', 'z2', 'z1', 'core'), pairs)  10.4 us
    pallas_call x1, Pallas kernels, precondition(): pl.pallas_call(precondition_kernel, out_shape=(jax.ShapeDtypeStruct((BLOC...  3.25 us
  transfers between devices with their start and end apart: 4, of which 4 were waited for; matrix products, arithmetic and copies ran while one was open for 0% of the time, Pallas kernels for 2%

profile of v5, /device:TPU:1, one launch (start us, length us, event | category | flops | bytes accessed | tf_op | source)
XLA Modules:
  0.0 117.1 jit_solution(16172214318244040124)
XLA Ops:
  0.0 1.6 %copy-done = bf16[1024,1024]{1,0:T(8,128)(2,1)S(1)} copy-done((bf16[1024,1024]{1,0:T(8,128)(2,1)S(1)}, bf16[1024,1024]{1,0:T(8,128)(2,1)}, u32[]{:S(2)}) %copy-start) | copy-done | bytes 2097176
  1.6 1.6 %gram.3 = f32[2112,128]{1,0:T(8,128)S(1)} custom-call(s32[1]{0:T(128)S(6)} %sub.3.share_ref, bf16[1024,1024]{1,0:T(8,128)(2,1)S(1)} %copy-done, bf16[1024,1024]{1,0:T(8,128)(2,1)S(1)} %copy-done), custom_call_target="tpu_custom_call" | custom-call | flops 805306368 | bytes 3145728 | tf_op jit(solution)/shard_map/gram/pallas_call | solution.py:83
  3.2 8.8 %collective-permute-start = (f32[2112,128]{1,0:T(8,128)S(1)}, f32[2112,128]{1,0:T(8,128)S(1)}, u32[]{:S(2)}, u32[]{:S(2)}) collective-permute-start(f32[2112,128]{1,0:T(8,128)S(1)} %gram.3), channel_id=1, source_target_pairs={{0,8},{8,0},{1,9},{9,1},{2,10},{10,2},{3,11},{11,3},{4,12},{12,4},... | collective-permute-start | bytes 3244040 | tf_op jit(solution)/shard_map/ppermute | solution.py:264
  12.0 0.0 copy-done.1
  12.0 1.6 %gram.2 = f32[2112,128]{1,0:T(8,128)S(1)} custom-call(s32[1]{0:T(128)} %bitcast.share_ref, bf16[1024,1024]{1,0:T(8,128)(2,1)S(1)} %copy-done.1, bf16[1024,1024]{1,0:T(8,128)(2,1)S(1)} %copy-done.1), custom_call_target="tpu_custom_call" | custom-call | flops 805306368 | bytes 3145728 | tf_op jit(solution)/shard_map/gram/pallas_call | solution.py:83
  13.6 0.7 collective-permute-done
  14.3 0.1 add.9
  14.4 18.3 %all_to_all.20 = f32[8,264,128]{2,1,0:T(8,128)S(1)} all-to-all(f32[8,264,128]{2,1,0:T(8,128)S(1)} %bitcast.7), channel_id=1, replica_groups=mesh['y'=4,'z4'=2,'z2'=2,'z1'=2,'core'=2,'x'=4,'z8'=2] {'z1','y'}, dimensions={0} | all-to-all | bytes 2162688 | tf_op jit(solution)/shard_map/all_to_all | solution.py:281
  32.7 0.1 reduce_sum.18
  32.8 6.0 %collective-permute-start.1 = (f32[264,128]{1,0:T(8,128)S(1)}, f32[264,128]{1,0:T(8,128)S(1)}, u32[]{:S(2)}, u32[]{:S(2)}) collective-permute-start(f32[264,128]{1,0:T(8,128)S(1)} %reduce_sum.18), channel_id=1, source_target_pairs={{0,32},{8,72},{16,48},{24,88},{32,0},{40,104},{48,16},{56,120},{64... | collective-permute-start | bytes 405512 | tf_op jit(solution)/shard_map/ppermute | solution.py:276
  38.8 6.8 %collective-permute-done.1 = f32[264,128]{1,0:T(8,128)S(1)} collective-permute-done((f32[264,128]{1,0:T(8,128)S(1)}, f32[264,128]{1,0:T(8,128)S(1)}, u32[]{:S(2)}, u32[]{:S(2)}) %collective-permute-start.1) | collective-permute-done | bytes 135200 | tf_op jit(solution)/shard_map/ppermute | solution.py:276
  45.7 4.4 %collective-permute-start.2 = (f32[264,128]{1,0:T(8,128)S(1)}, f32[264,128]{1,0:T(8,128)S(1)}, u32[]{:S(2)}, u32[]{:S(2)}) collective-permute-start(f32[264,128]{1,0:T(8,128)S(1)} %add.10), channel_id=1, source_target_pairs={{0,64},{8,40},{16,80},{24,56},{32,96},{40,8},{48,112},{56,24},{64,... | collective-permute-start | bytes 405512 | tf_op jit(solution)/shard_map/ppermute | solution.py:276
  50.1 6.0 %collective-permute-done.2 = f32[264,128]{1,0:T(8,128)S(1)} collective-permute-done((f32[264,128]{1,0:T(8,128)S(1)}, f32[264,128]{1,0:T(8,128)S(1)}, u32[]{:S(2)}, u32[]{:S(2)}) %collective-permute-start.2) | collective-permute-done | bytes 135200 | tf_op jit(solution)/shard_map/ppermute | solution.py:276
  56.1 0.1 broadcast_in_dim.4
  56.2 16.3 %all_to_all.21 = f32[8,264,128]{2,1,0:T(8,128)S(1)} all-to-all(f32[8,264,128]{2,1,0:T(8,128)S(1)} %broadcast_in_dim.4), channel_id=1, replica_groups=mesh['y'=4,'z4'=2,'z2'=2,'z1'=2,'core'=2,'x'=4,'z8'=2] {'z1','y'}, dimensions={0} | all-to-all | bytes 2162688 | tf_op jit(solution)/shard_map/all_to_all | solution.py:286
  72.6 5.4 %collective-permute-start.3 = (f32[2112,128]{1,0:T(8,128)S(1)}, f32[2112,128]{1,0:T(8,128)S(1)}, u32[]{:S(2)}, u32[]{:S(2)}) collective-permute-start(f32[2112,128]{1,0:T(8,128)S(1)} %bitcast.4), channel_id=1, source_target_pairs={{0,8},{8,0},{1,9},{9,1},{2,10},{10,2},{3,11},{11,3},{4,12},{12,4},... | collective-permute-start | bytes 3244040 | tf_op jit(solution)/shard_map/ppermute | solution.py:264
  78.0 0.6 unpack_own.1
  78.6 1.7 %collective-permute-done.3.other_ref = f32[2112,128]{1,0:T(8,128)S(1)} collective-permute-done((f32[2112,128]{1,0:T(8,128)S(1)}, f32[2112,128]{1,0:T(8,128)S(1)}, u32[]{:S(2)}, u32[]{:S(2)}) %collective-permute-start.3) | collective-permute-done | bytes 1081376 | tf_op jit(solution)/shard_map/ppermute | solution.py:264
  80.3 0.0 copy-done.2
  80.3 3.3 %precondition.1 = (bf16[1024,2048]{1,0:T(8,128)(2,1)S(1)}, f32[1024,128]{1,0:T(8,128)S(1)}, f32[32,1,128]{2,1,0:T(1,128)S(1)}) custom-call(s32[1]{0:T(128)} %bitcast.share_ref, bf16[1024,2048]{1,0:T(8,128)(2,1)S(1)} %get-tuple-element.9.half_factor_ref, f32[8,1024]{1,0:T(8,128)S(1)} %get-tuple-element.10.own_sums_ref, ...), custom_call_target="tpu_custom_call", output_to_operand_aliasing={{0}: (1, {})} | custom-call | flops 2415919104 | bytes 4194304 | tf_op jit(solution)/shard_map/precondition/pallas_call | solution.py:221
  83.5 12.4 %all_to_all.22 = f32[32,1,128]{2,1,0:T(1,128)S(1)} all-to-all(f32[32,1,128]{2,1,0:T(1,128)S(1)} %get-tuple-element.12), channel_id=1, replica_groups=mesh['y'=4,'z4'=2,'z2'=2,'z1'=2,'core'=2,'x'=4,'z8'=2] {'y','core','x'}, dimensions={0} | all-to-all | bytes 32768 | tf_op jit(solution)/shard_map/all_to_all | solution.py:302
  95.9 0.1 reduce_sum.19
  96.0 20.3 %all_to_all.23.align_ref = f32[16,1,128]{2,1,0:T(1,128)S(1)} all-to-all(f32[16,1,128]{2,1,0:T(1,128)S(1)} %broadcast_in_dim.5), channel_id=1, replica_groups=mesh['y'=4,'z4'=2,'z2'=2,'z1'=2,'core'=2,'x'=4,'z8'=2] {'z4','z2','z1','..., dimensions={0} | all-to-all | bytes 16384 | tf_op jit(solution)/shard_map/all_to_all | solution.py:304
  116.3 0.9 clip.1
  (8 shorter events, 0.1 us)
Async XLA Ops:
  0.0 1.6 %copy-start = (bf16[1024,1024]{1,0:T(8,128)(2,1)S(1)}, bf16[1024,1024]{1,0:T(8,128)(2,1)}, u32[]{:S(2)}) copy-start(bf16[1024,1024]{1,0:T(8,128)(2,1)} %other_ref.3) | copy-start | bytes 6291460
  1.6 10.4 %copy-start.1 = (bf16[1024,1024]{1,0:T(8,128)(2,1)S(1)}, bf16[1024,1024]{1,0:T(8,128)(2,1)}, u32[]{:S(2)}) copy-start(bf16[1024,1024]{1,0:T(8,128)(2,1)} %other_ref.3) | copy-start | bytes 6291460
  3.2 11.1 %collective-permute-start = (f32[2112,128]{1,0:T(8,128)S(1)}, f32[2112,128]{1,0:T(8,128)S(1)}, u32[]{:S(2)}, u32[]{:S(2)}) collective-permute-start(f32[2112,128]{1,0:T(8,128)S(1)} %gram.3), channel_id=1, source_target_pairs={{0,8},{8,0},{1,9},{9,1},{2,10},{10,2},{3,11},{11,3},{4,12},{12,4},... | collective-permute-start | bytes 3244040 | tf_op jit(solution)/shard_map/ppermute | solution.py:264
  32.8 12.9 %collective-permute-start.1 = (f32[264,128]{1,0:T(8,128)S(1)}, f32[264,128]{1,0:T(8,128)S(1)}, u32[]{:S(2)}, u32[]{:S(2)}) collective-permute-start(f32[264,128]{1,0:T(8,128)S(1)} %reduce_sum.18), channel_id=1, source_target_pairs={{0,32},{8,72},{16,48},{24,88},{32,0},{40,104},{48,16},{56,120},{64... | collective-permute-start | bytes 405512 | tf_op jit(solution)/shard_map/ppermute | solution.py:276
  45.7 10.4 %collective-permute-start.2 = (f32[264,128]{1,0:T(8,128)S(1)}, f32[264,128]{1,0:T(8,128)S(1)}, u32[]{:S(2)}, u32[]{:S(2)}) collective-permute-start(f32[264,128]{1,0:T(8,128)S(1)} %add.10), channel_id=1, source_target_pairs={{0,64},{8,40},{16,80},{24,56},{32,96},{40,8},{48,112},{56,24},{64,... | collective-permute-start | bytes 405512 | tf_op jit(solution)/shard_map/ppermute | solution.py:276
  72.6 7.7 %copy-start.2 = (bf16[1024,128]{1,0:T(8,128)(2,1)S(1)}, bf16[1024,128]{1,0:T(8,128)(2,1)}, u32[]{:S(2)}) copy-start(bf16[1024,128]{1,0:T(8,128)(2,1)} %grad_ref.1) | copy-start | bytes 786436
  72.6 7.7 %copy-start.3 = (f32[128]{0:T(128)S(1)}, f32[128]{0:T(128)}, u32[]{:S(2)}) copy-start(f32[128]{0:T(128)} %param.5) | copy-start | bytes 1540
  72.6 7.7 %collective-permute-start.3 = (f32[2112,128]{1,0:T(8,128)S(1)}, f32[2112,128]{1,0:T(8,128)S(1)}, u32[]{:S(2)}, u32[]{:S(2)}) collective-permute-start(f32[2112,128]{1,0:T(8,128)S(1)} %bitcast.4), channel_id=1, source_target_pairs={{0,8},{8,0},{1,9},{9,1},{2,10},{10,2},{3,11},{11,3},{4,12},{12,4},... | collective-permute-start | bytes 3244040 | tf_op jit(solution)/shard_map/ppermute | solution.py:264

commit v6 on v5

--- a/solution.py
+++ b/solution.py
@@ -41,7 +41,7 @@
     return 2 + 3 * i + d - 1
 
 
-def gram_kernel(share_ref, own_ref, other_ref, out_ref):
+def gram_kernel(share_ref, activations_ref, out_ref):
     share = share_ref[0]
     row, column = row_and_column()
 
@@ -50,8 +50,8 @@
             lhs, rhs, (((0,), (0,)), ((), ())), preferred_element_type=f32
         )
 
-    own = own_ref[...]
-    other = other_ref[...]
+    own = activations_ref[:, pl.ds(pl.multiple_of(share * HALF, HALF), HALF)]
+    other = activations_ref[:, pl.ds(pl.multiple_of((1 - share) * HALF, HALF), HALF)]
     out_ref[DIAGONALS:, :] = jnp.zeros((SHARE - DIAGONALS, TILE), f32)
     for pair in range(2):
         lhs = own[:, pair * 256 : (pair + 1) * 256]
@@ -83,21 +83,17 @@
     return pl.pallas_call(
         gram_kernel,
         out_shape=jax.ShapeDtypeStruct((SHARE, TILE), f32),
-        grid_spec=pltpu.PrefetchScalarGridSpec(
-            num_scalar_prefetch=1,
-            grid=(1,),
-            in_specs=[
-                pl.BlockSpec((tokens, HALF), lambda g, s: (0, s[0])),
-                pl.BlockSpec((tokens, HALF), lambda g, s: (0, 1 - s[0])),
-            ],
-            out_specs=pl.BlockSpec((SHARE, TILE), lambda g, s: (0, 0)),
-        ),
+        in_specs=[
+            pl.BlockSpec(memory_space=pltpu.SMEM),
+            pl.BlockSpec(memory_space=pltpu.VMEM),
+        ],
+        out_specs=pl.BlockSpec(memory_space=pltpu.VMEM),
         compiler_params=pltpu.CompilerParams(vmem_limit_bytes=24 * 2**20),
         cost_estimate=pl.CostEstimate(
             flops=2 * tokens * 512 * 768, bytes_accessed=3 * 2**20, transcendentals=0
         ),
         name="gram",
-    )(share, activations, activations)
+    )(share, activations)
 
 
 def put(factor_ref, sums_ref, tile, i, j):

time: 118 us -> 117 us (level)
  no operation moved by 1% of the time
where the time goes in v6:
time: 117 us
  blocking collectives  67.3 us (58%)
  starting transfers between devices  24.6 us (21%)
  waiting for transfers between devices  15.3 us (13%)
  Pallas kernels  7.77 us (7%)
  local copies, waits for them, and re-layouts  1.68 us (1%)
    all_to_all x1, blocking collectives, on_device(): lanes = lax.all_to_all(lanes, ('z4', 'z2', 'z1', 'z8'), 0, 0)  20 us
    all_to_all x1, blocking collectives, scatter_sum(): return jnp.sum(lax.all_to_all(pieces, axes, 0, 0), axis=0)  18.3 us
    all_to_all x1, blocking collectives, gather(): lax.all_to_all(copies, axes, 0, 0).reshape(parts * x.shape[0], x.shape[1])  16.3 us
    ppermute x2, starting transfers between devices, swap(): return lax.ppermute(x, axis, [(0, 1), (1, 0)])  14.2 us
    ppermute x2, waiting for transfers between devices, cross(): return lax.ppermute(x, ('z4', 'z2', 'z1', 'core'), pairs)  12.9 us
    all_to_all x1, blocking collectives, on_device(): lanes = jnp.sum(lax.all_to_all(align, ('y', 'core', 'x'), 0, 0), axis=0)  12.6 us
    ppermute x2, starting transfers between devices, cross(): return lax.ppermute(x, ('z4', 'z2', 'z1', 'core'), pairs)  10.5 us
    pallas_call x1, Pallas kernels, precondition(): pl.pallas_call(precondition_kernel, out_shape=(jax.ShapeDtypeStruct((BLOC...  3.24 us
  transfers between devices with their start and end apart: 4, of which 4 were waited for; matrix products, arithmetic and copies ran while one was open for 0% of the time, Pallas kernels for 2%

profile of v6, /device:TPU:1, one launch (start us, length us, event | category | flops | bytes accessed | tf_op | source)
XLA Modules:
  0.0 117.1 jit_solution(9060365507654361822)
XLA Ops:
  0.0 1.6 %copy-done = bf16[1024,1024]{1,0:T(8,128)(2,1)S(1)} copy-done((bf16[1024,1024]{1,0:T(8,128)(2,1)S(1)}, bf16[1024,1024]{1,0:T(8,128)(2,1)}, u32[]{:S(2)}) %copy-start) | copy-done | bytes 2097176
  1.6 1.5 %gram.3 = f32[2112,128]{1,0:T(8,128)S(1)} custom-call(s32[1]{0:T(128)S(6)} %sub.3.share_ref, bf16[1024,1024]{1,0:T(8,128)(2,1)S(1)} %copy-done), custom_call_target="tpu_custom_call" | custom-call | flops 805306368 | bytes 3145728 | tf_op jit(solution)/shard_map/gram/pallas_call | solution.py:83
  3.1 8.8 %collective-permute-start = (f32[2112,128]{1,0:T(8,128)S(1)}, f32[2112,128]{1,0:T(8,128)S(1)}, u32[]{:S(2)}, u32[]{:S(2)}) collective-permute-start(f32[2112,128]{1,0:T(8,128)S(1)} %gram.3), channel_id=1, source_target_pairs={{0,8},{8,0},{1,9},{9,1},{2,10},{10,2},{3,11},{11,3},{4,12},{12,4},... | collective-permute-start | bytes 3244040 | tf_op jit(solution)/shard_map/ppermute | solution.py:260
  11.9 0.0 copy-done.1
  11.9 1.5 %gram.2 = f32[2112,128]{1,0:T(8,128)S(1)} custom-call(s32[1]{0:T(128)} %bitcast.share_ref, bf16[1024,1024]{1,0:T(8,128)(2,1)S(1)} %copy-done.1), custom_call_target="tpu_custom_call" | custom-call | flops 805306368 | bytes 3145728 | tf_op jit(solution)/shard_map/gram/pallas_call | solution.py:83
  13.5 0.8 collective-permute-done
  14.2 0.1 add.9
  14.3 18.3 %all_to_all.20 = f32[8,264,128]{2,1,0:T(8,128)S(1)} all-to-all(f32[8,264,128]{2,1,0:T(8,128)S(1)} %bitcast.7), channel_id=1, replica_groups=mesh['y'=4,'z4'=2,'z2'=2,'z1'=2,'core'=2,'x'=4,'z8'=2] {'z1','y'}, dimensions={0} | all-to-all | bytes 2162688 | tf_op jit(solution)/shard_map/all_to_all | solution.py:277
  32.7 0.1 reduce_sum.18
  32.7 6.1 %collective-permute-start.1 = (f32[264,128]{1,0:T(8,128)S(1)}, f32[264,128]{1,0:T(8,128)S(1)}, u32[]{:S(2)}, u32[]{:S(2)}) collective-permute-start(f32[264,128]{1,0:T(8,128)S(1)} %reduce_sum.18), channel_id=1, source_target_pairs={{0,32},{8,72},{16,48},{24,88},{32,0},{40,104},{48,16},{56,120},{64... | collective-permute-start | bytes 405512 | tf_op jit(solution)/shard_map/ppermute | solution.py:272
  38.8 6.8 %collective-permute-done.1 = f32[264,128]{1,0:T(8,128)S(1)} collective-permute-done((f32[264,128]{1,0:T(8,128)S(1)}, f32[264,128]{1,0:T(8,128)S(1)}, u32[]{:S(2)}, u32[]{:S(2)}) %collective-permute-start.1) | collective-permute-done | bytes 135200 | tf_op jit(solution)/shard_map/ppermute | solution.py:272
  45.6 4.4 %collective-permute-start.2 = (f32[264,128]{1,0:T(8,128)S(1)}, f32[264,128]{1,0:T(8,128)S(1)}, u32[]{:S(2)}, u32[]{:S(2)}) collective-permute-start(f32[264,128]{1,0:T(8,128)S(1)} %add.10), channel_id=1, source_target_pairs={{0,64},{8,40},{16,80},{24,56},{32,96},{40,8},{48,112},{56,24},{64,... | collective-permute-start | bytes 405512 | tf_op jit(solution)/shard_map/ppermute | solution.py:272
  50.0 6.0 %collective-permute-done.2 = f32[264,128]{1,0:T(8,128)S(1)} collective-permute-done((f32[264,128]{1,0:T(8,128)S(1)}, f32[264,128]{1,0:T(8,128)S(1)}, u32[]{:S(2)}, u32[]{:S(2)}) %collective-permute-start.2) | collective-permute-done | bytes 135200 | tf_op jit(solution)/shard_map/ppermute | solution.py:272
  56.1 0.1 broadcast_in_dim.4
  56.2 16.3 %all_to_all.21 = f32[8,264,128]{2,1,0:T(8,128)S(1)} all-to-all(f32[8,264,128]{2,1,0:T(8,128)S(1)} %broadcast_in_dim.4), channel_id=1, replica_groups=mesh['y'=4,'z4'=2,'z2'=2,'z1'=2,'core'=2,'x'=4,'z8'=2] {'z1','y'}, dimensions={0} | all-to-all | bytes 2162688 | tf_op jit(solution)/shard_map/all_to_all | solution.py:282
  72.5 5.4 %collective-permute-start.3 = (f32[2112,128]{1,0:T(8,128)S(1)}, f32[2112,128]{1,0:T(8,128)S(1)}, u32[]{:S(2)}, u32[]{:S(2)}) collective-permute-start(f32[2112,128]{1,0:T(8,128)S(1)} %bitcast.4), channel_id=1, source_target_pairs={{0,8},{8,0},{1,9},{9,1},{2,10},{10,2},{3,11},{11,3},{4,12},{12,4},... | collective-permute-start | bytes 3244040 | tf_op jit(solution)/shard_map/ppermute | solution.py:260
  77.9 0.6 unpack_own.1
  78.5 1.7 %collective-permute-done.3.other_ref = f32[2112,128]{1,0:T(8,128)S(1)} collective-permute-done((f32[2112,128]{1,0:T(8,128)S(1)}, f32[2112,128]{1,0:T(8,128)S(1)}, u32[]{:S(2)}, u32[]{:S(2)}) %collective-permute-start.3) | collective-permute-done | bytes 1081376 | tf_op jit(solution)/shard_map/ppermute | solution.py:260
  80.2 0.0 copy-done.3
  80.2 3.2 %precondition.1 = (bf16[1024,2048]{1,0:T(8,128)(2,1)S(1)}, f32[1024,128]{1,0:T(8,128)S(1)}, f32[32,1,128]{2,1,0:T(1,128)S(1)}) custom-call(s32[1]{0:T(128)} %bitcast.share_ref, bf16[1024,2048]{1,0:T(8,128)(2,1)S(1)} %get-tuple-element.9.half_factor_ref, f32[8,1024]{1,0:T(8,128)S(1)} %get-tuple-element.10.own_sums_ref, ...), custom_call_target="tpu_custom_call", output_to_operand_aliasing={{0}: (1, {})} | custom-call | flops 2415919104 | bytes 4194304 | tf_op jit(solution)/shard_map/precondition/pallas_call | solution.py:217
  83.5 12.6 %all_to_all.22 = f32[32,1,128]{2,1,0:T(1,128)S(1)} all-to-all(f32[32,1,128]{2,1,0:T(1,128)S(1)} %get-tuple-element.12), channel_id=1, replica_groups=mesh['y'=4,'z4'=2,'z2'=2,'z1'=2,'core'=2,'x'=4,'z8'=2] {'y','core','x'}, dimensions={0} | all-to-all | bytes 32768 | tf_op jit(solution)/shard_map/all_to_all | solution.py:298
  96.1 0.1 reduce_sum.19
  96.2 20.0 %all_to_all.23.align_ref = f32[16,1,128]{2,1,0:T(1,128)S(1)} all-to-all(f32[16,1,128]{2,1,0:T(1,128)S(1)} %broadcast_in_dim.5), channel_id=1, replica_groups=mesh['y'=4,'z4'=2,'z2'=2,'z1'=2,'core'=2,'x'=4,'z8'=2] {'z4','z2','z1','..., dimensions={0} | all-to-all | bytes 16384 | tf_op jit(solution)/shard_map/all_to_all | solution.py:300
  116.2 0.9 clip.1
  (8 shorter events, 0.1 us)
Async XLA Ops:
  0.0 1.6 %copy-start = (bf16[1024,1024]{1,0:T(8,128)(2,1)S(1)}, bf16[1024,1024]{1,0:T(8,128)(2,1)}, u32[]{:S(2)}) copy-start(bf16[1024,1024]{1,0:T(8,128)(2,1)} %activations_ref.3) | copy-start | bytes 6291460
  1.6 10.3 %copy-start.1 = (bf16[1024,1024]{1,0:T(8,128)(2,1)S(1)}, bf16[1024,1024]{1,0:T(8,128)(2,1)}, u32[]{:S(2)}) copy-start(bf16[1024,1024]{1,0:T(8,128)(2,1)} %activations_ref.3) | copy-start | bytes 6291460
  3.1 11.1 %collective-permute-start = (f32[2112,128]{1,0:T(8,128)S(1)}, f32[2112,128]{1,0:T(8,128)S(1)}, u32[]{:S(2)}, u32[]{:S(2)}) collective-permute-start(f32[2112,128]{1,0:T(8,128)S(1)} %gram.3), channel_id=1, source_target_pairs={{0,8},{8,0},{1,9},{9,1},{2,10},{10,2},{3,11},{11,3},{4,12},{12,4},... | collective-permute-start | bytes 3244040 | tf_op jit(solution)/shard_map/ppermute | solution.py:260
  32.7 12.9 %collective-permute-start.1 = (f32[264,128]{1,0:T(8,128)S(1)}, f32[264,128]{1,0:T(8,128)S(1)}, u32[]{:S(2)}, u32[]{:S(2)}) collective-permute-start(f32[264,128]{1,0:T(8,128)S(1)} %reduce_sum.18), channel_id=1, source_target_pairs={{0,32},{8,72},{16,48},{24,88},{32,0},{40,104},{48,16},{56,120},{64... | collective-permute-start | bytes 405512 | tf_op jit(solution)/shard_map/ppermute | solution.py:272
  45.6 10.4 %collective-permute-start.2 = (f32[264,128]{1,0:T(8,128)S(1)}, f32[264,128]{1,0:T(8,128)S(1)}, u32[]{:S(2)}, u32[]{:S(2)}) collective-permute-start(f32[264,128]{1,0:T(8,128)S(1)} %add.10), channel_id=1, source_target_pairs={{0,64},{8,40},{16,80},{24,56},{32,96},{40,8},{48,112},{56,24},{64,... | collective-permute-start | bytes 405512 | tf_op jit(solution)/shard_map/ppermute | solution.py:272
  72.5 7.7 %copy-start.2 = (bf16[1024,128]{1,0:T(8,128)(2,1)S(1)}, bf16[1024,128]{1,0:T(8,128)(2,1)}, u32[]{:S(2)}) copy-start(bf16[1024,128]{1,0:T(8,128)(2,1)} %grad_ref.1) | copy-start | bytes 786436
  72.5 7.7 %copy-start.3 = (f32[128]{0:T(128)S(1)}, f32[128]{0:T(128)}, u32[]{:S(2)}) copy-start(f32[128]{0:T(128)} %param.5) | copy-start | bytes 1540
  72.5 7.7 %collective-permute-start.3 = (f32[2112,128]{1,0:T(8,128)S(1)}, f32[2112,128]{1,0:T(8,128)S(1)}, u32[]{:S(2)}, u32[]{:S(2)}) collective-permute-start(f32[2112,128]{1,0:T(8,128)S(1)} %bitcast.4), channel_id=1, source_target_pairs={{0,8},{8,0},{1,9},{9,1},{2,10},{10,2},{3,11},{11,3},{4,12},{12,4},... | collective-permute-start | bytes 3244040 | tf_op jit(solution)/shard_map/ppermute | solution.py:260

commit v7 on v5

--- a/solution.py
+++ b/solution.py
@@ -19,10 +19,10 @@
 damping = 0.1
 kl_bound = 2.0
 
-AXES = ("y", "z4", "z2", "z1", "core", "x", "z8")
-SIZES = (4, 2, 2, 2, 2, 4, 2)
-DP = AXES[:5]
-MP = AXES[5:]
+AXES = ("y2", "y1", "z4", "z2", "z1", "core", "x", "z8")
+SIZES = (2, 2, 2, 2, 2, 2, 4, 2)
+DP = AXES[:6]
+MP = AXES[6:]
 
 f32 = jnp.float32
 bf16 = jnp.bfloat16
@@ -292,14 +292,14 @@
     theirs = 1 - mine
     away = swap(gram(theirs, activations), "core")
     chip = gram(mine, activations) + away
-    part = scatter_sum(chip, ("z1", "y"), 8)
+    part = scatter_sum(chip, ("y2", "z1", "y1"), 8)
     part = part + cross(part, 0)
     part = part + cross(part, 1)
-    own = gather(part, ("z1", "y"), 8)
+    own = gather(part, ("y2", "z1", "y1"), 8)
     other = swap(own, "core")
     half_factor, own_sums = unpack_own(mine, own)
     scaled, align = precondition(mine, half_factor, own_sums, other, gradient, out_scale, 32)
-    lanes = jnp.sum(lax.all_to_all(align, ("y", "core", "x"), 0, 0), axis=0)
+    lanes = jnp.sum(lax.all_to_all(align, ("y2", "y1", "core", "x"), 0, 0), axis=0)
     lanes = jnp.broadcast_to(lanes[None], (16, 1, COLS))
     lanes = lax.all_to_all(lanes, ("z4", "z2", "z1", "z8"), 0, 0)
     return clip(scaled, lanes)

time: 118 us -> 117 us (level)
  waiting for transfers between devices: 15.3 us -> 13.8 us
  starting transfers between devices: 24.6 us -> 25.8 us
    ppermute x2, waiting for transfers between devices: 12.9 us -> 11.4 us  [cross(): return lax.ppermute(x, ('z4', 'z2', 'z1', 'core'), pairs)]
    ppermute x2, starting transfers between devices: 14.2 us -> 15.4 us  [swap(): return lax.ppermute(x, axis, [(0, 1), (1, 0)])]
where the time goes in v7:
time: 117 us
  blocking collectives  67.5 us (58%)
  starting transfers between devices  25.8 us (22%)
  waiting for transfers between devices  13.8 us (12%)
  Pallas kernels  7.85 us (7%)
  local copies, waits for them, and re-layouts  1.68 us (1%)
    all_to_all x1, blocking collectives, on_device(): lanes = lax.all_to_all(lanes, ('z4', 'z2', 'z1', 'z8'), 0, 0)  20.2 us
    all_to_all x1, blocking collectives, scatter_sum(): return jnp.sum(lax.all_to_all(pieces, axes, 0, 0), axis=0)  18.2 us
    all_to_all x1, blocking collectives, gather(): lax.all_to_all(copies, axes, 0, 0).reshape(parts * x.shape[0], x.shape[1])  16.3 us
    ppermute x2, starting transfers between devices, swap(): return lax.ppermute(x, axis, [(0, 1), (1, 0)])  15.4 us
    all_to_all x1, blocking collectives, on_device(): lax.all_to_all(align, ('y2', 'y1', 'core', 'x'), 0, 0)  12.8 us
    ppermute x2, waiting for transfers between devices, cross(): return lax.ppermute(x, ('z4', 'z2', 'z1', 'core'), pairs)  11.4 us
    ppermute x2, starting transfers between devices, cross(): return lax.ppermute(x, ('z4', 'z2', 'z1', 'core'), pairs)  10.4 us
    pallas_call x1, Pallas kernels, precondition(): pl.pallas_call(precondition_kernel, out_shape=(jax.ShapeDtypeStruct((BLOC...  3.25 us
  transfers between devices with their start and end apart: 4, of which 4 were waited for; matrix products, arithmetic and copies ran while one was open for 0% of the time, Pallas kernels for 2%

profile of v7, /device:TPU:1, one launch (start us, length us, event | category | flops | bytes accessed | tf_op | source)
XLA Modules:
  0.0 116.9 jit_solution(1826564222193074394)
XLA Ops:
  0.0 1.6 %copy-done = bf16[1024,1024]{1,0:T(8,128)(2,1)S(1)} copy-done((bf16[1024,1024]{1,0:T(8,128)(2,1)S(1)}, bf16[1024,1024]{1,0:T(8,128)(2,1)}, u32[]{:S(2)}) %copy-start) | copy-done | bytes 2097176
  1.6 1.6 %gram.3 = f32[2112,128]{1,0:T(8,128)S(1)} custom-call(s32[1]{0:T(128)S(6)} %sub.3.share_ref, bf16[1024,1024]{1,0:T(8,128)(2,1)S(1)} %copy-done, bf16[1024,1024]{1,0:T(8,128)(2,1)S(1)} %copy-done), custom_call_target="tpu_custom_call" | custom-call | flops 805306368 | bytes 3145728 | tf_op jit(solution)/shard_map/gram/pallas_call | solution.py:83
  3.2 8.8 %collective-permute-start = (f32[2112,128]{1,0:T(8,128)S(1)}, f32[2112,128]{1,0:T(8,128)S(1)}, u32[]{:S(2)}, u32[]{:S(2)}) collective-permute-start(f32[2112,128]{1,0:T(8,128)S(1)} %gram.3), channel_id=1, source_target_pairs={{0,8},{8,0},{1,9},{9,1},{2,10},{10,2},{3,11},{11,3},{4,12},{12,4},... | collective-permute-start | bytes 3244040 | tf_op jit(solution)/shard_map/ppermute | solution.py:264
  12.0 0.0 copy-done.1
  12.0 1.6 %gram.2 = f32[2112,128]{1,0:T(8,128)S(1)} custom-call(s32[1]{0:T(128)} %bitcast.share_ref, bf16[1024,1024]{1,0:T(8,128)(2,1)S(1)} %copy-done.1, bf16[1024,1024]{1,0:T(8,128)(2,1)S(1)} %copy-done.1), custom_call_target="tpu_custom_call" | custom-call | flops 805306368 | bytes 3145728 | tf_op jit(solution)/shard_map/gram/pallas_call | solution.py:83
  13.6 0.7 collective-permute-done
  14.3 0.1 add.9
  14.4 18.2 %all_to_all.20 = f32[8,264,128]{2,1,0:T(8,128)S(1)} all-to-all(f32[8,264,128]{2,1,0:T(8,128)S(1)} %bitcast.7), channel_id=1, replica_groups=mesh['y2'=2,'y1'=2,'z4'=2,'z2'=2,'z1'=2,'core'=2,'x'=4,'z8'=2] {'y2','z1..., dimensions={0} | all-to-all | bytes 2162688 | tf_op jit(solution)/shard_map/all_to_all | solution.py:281
  32.6 0.1 reduce_sum.18
  32.7 6.1 %collective-permute-start.1 = (f32[264,128]{1,0:T(8,128)S(1)}, f32[264,128]{1,0:T(8,128)S(1)}, u32[]{:S(2)}, u32[]{:S(2)}) collective-permute-start(f32[264,128]{1,0:T(8,128)S(1)} %reduce_sum.18), channel_id=1, source_target_pairs={{0,32},{8,72},{16,48},{24,88},{32,0},{40,104},{48,16},{56,120},{64... | collective-permute-start | bytes 405512 | tf_op jit(solution)/shard_map/ppermute | solution.py:276
  38.8 6.9 %collective-permute-done.1 = f32[264,128]{1,0:T(8,128)S(1)} collective-permute-done((f32[264,128]{1,0:T(8,128)S(1)}, f32[264,128]{1,0:T(8,128)S(1)}, u32[]{:S(2)}, u32[]{:S(2)}) %collective-permute-start.1) | collective-permute-done | bytes 135200 | tf_op jit(solution)/shard_map/ppermute | solution.py:276
  45.7 4.3 %collective-permute-start.2 = (f32[264,128]{1,0:T(8,128)S(1)}, f32[264,128]{1,0:T(8,128)S(1)}, u32[]{:S(2)}, u32[]{:S(2)}) collective-permute-start(f32[264,128]{1,0:T(8,128)S(1)} %add.10), channel_id=1, source_target_pairs={{0,64},{8,40},{16,80},{24,56},{32,96},{40,8},{48,112},{56,24},{64,... | collective-permute-start | bytes 405512 | tf_op jit(solution)/shard_map/ppermute | solution.py:276
  50.0 4.4 %collective-permute-done.2 = f32[264,128]{1,0:T(8,128)S(1)} collective-permute-done((f32[264,128]{1,0:T(8,128)S(1)}, f32[264,128]{1,0:T(8,128)S(1)}, u32[]{:S(2)}, u32[]{:S(2)}) %collective-permute-start.2) | collective-permute-done | bytes 135200 | tf_op jit(solution)/shard_map/ppermute | solution.py:276
  54.4 0.1 broadcast_in_dim.4
  54.5 16.3 %all_to_all.21 = f32[8,264,128]{2,1,0:T(8,128)S(1)} all-to-all(f32[8,264,128]{2,1,0:T(8,128)S(1)} %broadcast_in_dim.4), channel_id=1, replica_groups=mesh['y2'=2,'y1'=2,'z4'=2,'z2'=2,'z1'=2,'core'=2,'x'=4,'z8'=2] {'y2','z1..., dimensions={0} | all-to-all | bytes 2162688 | tf_op jit(solution)/shard_map/all_to_all | solution.py:286
  70.8 6.6 %collective-permute-start.3 = (f32[2112,128]{1,0:T(8,128)S(1)}, f32[2112,128]{1,0:T(8,128)S(1)}, u32[]{:S(2)}, u32[]{:S(2)}) collective-permute-start(f32[2112,128]{1,0:T(8,128)S(1)} %bitcast.4), channel_id=1, source_target_pairs={{0,8},{8,0},{1,9},{9,1},{2,10},{10,2},{3,11},{11,3},{4,12},{12,4},... | collective-permute-start | bytes 3244040 | tf_op jit(solution)/shard_map/ppermute | solution.py:264
  77.4 0.6 unpack_own.1
  78.1 1.7 %collective-permute-done.3.other_ref = f32[2112,128]{1,0:T(8,128)S(1)} collective-permute-done((f32[2112,128]{1,0:T(8,128)S(1)}, f32[2112,128]{1,0:T(8,128)S(1)}, u32[]{:S(2)}, u32[]{:S(2)}) %collective-permute-start.3) | collective-permute-done | bytes 1081376 | tf_op jit(solution)/shard_map/ppermute | solution.py:264
  79.8 0.0 copy-done.2
  79.8 3.2 %precondition.1 = (bf16[1024,2048]{1,0:T(8,128)(2,1)S(1)}, f32[1024,128]{1,0:T(8,128)S(1)}, f32[32,1,128]{2,1,0:T(1,128)S(1)}) custom-call(s32[1]{0:T(128)} %bitcast.share_ref, bf16[1024,2048]{1,0:T(8,128)(2,1)S(1)} %get-tuple-element.9.half_factor_ref, f32[8,1024]{1,0:T(8,128)S(1)} %get-tuple-element.10.own_sums_ref, ...), custom_call_target="tpu_custom_call", output_to_operand_aliasing={{0}: (1, {})} | custom-call | flops 2415919104 | bytes 4194304 | tf_op jit(solution)/shard_map/precondition/pallas_call | solution.py:221
  83.0 12.8 %all_to_all.22 = f32[32,1,128]{2,1,0:T(1,128)S(1)} all-to-all(f32[32,1,128]{2,1,0:T(1,128)S(1)} %get-tuple-element.12), channel_id=1, replica_groups=mesh['y2'=2,'y1'=2,'z4'=2,'z2'=2,'z1'=2,'core'=2,'x'=4,'z8'=2] {'y2','y1..., dimensions={0} | all-to-all | bytes 32768 | tf_op jit(solution)/shard_map/all_to_all | solution.py:302
  95.8 0.1 reduce_sum.19
  95.9 20.2 %all_to_all.23.align_ref = f32[16,1,128]{2,1,0:T(1,128)S(1)} all-to-all(f32[16,1,128]{2,1,0:T(1,128)S(1)} %broadcast_in_dim.5), channel_id=1, replica_groups=mesh['y2'=2,'y1'=2,'z4'=2,'z2'=2,'z1'=2,'core'=2,'x'=4,'z8'=2] {'z4','z2..., dimensions={0} | all-to-all | bytes 16384 | tf_op jit(solution)/shard_map/all_to_all | solution.py:304
  116.1 0.9 clip.1
  (8 shorter events, 0.1 us)
Async XLA Ops:
  0.0 1.6 %copy-start = (bf16[1024,1024]{1,0:T(8,128)(2,1)S(1)}, bf16[1024,1024]{1,0:T(8,128)(2,1)}, u32[]{:S(2)}) copy-start(bf16[1024,1024]{1,0:T(8,128)(2,1)} %other_ref.3) | copy-start | bytes 6291460
  1.6 10.4 %copy-start.1 = (bf16[1024,1024]{1,0:T(8,128)(2,1)S(1)}, bf16[1024,1024]{1,0:T(8,128)(2,1)}, u32[]{:S(2)}) copy-start(bf16[1024,1024]{1,0:T(8,128)(2,1)} %other_ref.3) | copy-start | bytes 6291460
  3.2 11.1 %collective-permute-start = (f32[2112,128]{1,0:T(8,128)S(1)}, f32[2112,128]{1,0:T(8,128)S(1)}, u32[]{:S(2)}, u32[]{:S(2)}) collective-permute-start(f32[2112,128]{1,0:T(8,128)S(1)} %gram.3), channel_id=1, source_target_pairs={{0,8},{8,0},{1,9},{9,1},{2,10},{10,2},{3,11},{11,3},{4,12},{12,4},... | collective-permute-start | bytes 3244040 | tf_op jit(solution)/shard_map/ppermute | solution.py:264
  32.7 13.0 %collective-permute-start.1 = (f32[264,128]{1,0:T(8,128)S(1)}, f32[264,128]{1,0:T(8,128)S(1)}, u32[]{:S(2)}, u32[]{:S(2)}) collective-permute-start(f32[264,128]{1,0:T(8,128)S(1)} %reduce_sum.18), channel_id=1, source_target_pairs={{0,32},{8,72},{16,48},{24,88},{32,0},{40,104},{48,16},{56,120},{64... | collective-permute-start | bytes 405512 | tf_op jit(solution)/shard_map/ppermute | solution.py:276
  45.7 8.7 %collective-permute-start.2 = (f32[264,128]{1,0:T(8,128)S(1)}, f32[264,128]{1,0:T(8,128)S(1)}, u32[]{:S(2)}, u32[]{:S(2)}) collective-permute-start(f32[264,128]{1,0:T(8,128)S(1)} %add.10), channel_id=1, source_target_pairs={{0,64},{8,40},{16,80},{24,56},{32,96},{40,8},{48,112},{56,24},{64,... | collective-permute-start | bytes 405512 | tf_op jit(solution)/shard_map/ppermute | solution.py:276
  70.8 9.0 %copy-start.2 = (bf16[1024,128]{1,0:T(8,128)(2,1)S(1)}, bf16[1024,128]{1,0:T(8,128)(2,1)}, u32[]{:S(2)}) copy-start(bf16[1024,128]{1,0:T(8,128)(2,1)} %grad_ref.1) | copy-start | bytes 786436
  70.8 9.0 %copy-start.3 = (f32[128]{0:T(128)S(1)}, f32[128]{0:T(128)}, u32[]{:S(2)}) copy-start(f32[128]{0:T(128)} %param.5) | copy-start | bytes 1540
  70.8 8.9 %collective-permute-start.3 = (f32[2112,128]{1,0:T(8,128)S(1)}, f32[2112,128]{1,0:T(8,128)S(1)}, u32[]{:S(2)}, u32[]{:S(2)}) collective-permute-start(f32[2112,128]{1,0:T(8,128)S(1)} %bitcast.4), channel_id=1, source_target_pairs={{0,8},{8,0},{1,9},{9,1},{2,10},{10,2},{3,11},{11,3},{4,12},{12,4},... | collective-permute-start | bytes 3244040 | tf_op jit(solution)/shard_map/ppermute | solution.py:264
